TPU v7x, 32 devices: a whole 2x2x4 slice. The times are simulated.
32 devices in a mesh: dp: 8 (over z, x), mod: 4 (over y, core).
Axes of the slice: x: 2, y: 2, z: 4, core: 2. Of those that a mesh axis runs over, the one named last changes fastest.
Arguments:
- tokens: bfloat16 [64, 256, 1152], P(('dp', 'mod')), may hold values from -6 to 6
- condition: bfloat16 [64, 1152], P(('dp', 'mod')), may hold values from -6 to 6
- timestep: int32 [64], P(('dp', 'mod')), may hold values from 0 to 999
- qkv_weight: bfloat16 [1152, 3456], P('dp'), may hold values from -0.1875 to 0.1875
- out_weight: bfloat16 [1152, 1152], P('dp'), may hold values from -1.5 to 1.5
- gate_weight: bfloat16 [1152, 3072], P('dp'), may hold values from -0.1875 to 0.1875
- up_weight: bfloat16 [1152, 3072], P('dp'), may hold values from -0.1875 to 0.1875
- down_weight: bfloat16 [3072, 1152], P('dp'), may hold values from -0.109375 to 0.109375
- mod_weight: bfloat16 [1152, 6912], P(None, 'mod'), may hold values from -0.1875 to 0.1875
- mod_bias: bfloat16 [6912], P('mod'), may hold values from -3 to 3
- cotangent: bfloat16 [64, 256, 1152], P(('dp', 'mod')), may hold values from -6 to 6
Outputs:
- output_tokens: bfloat16 [64, 256, 1152], P(('dp', 'mod'))
- grad_tokens: float32 [64, 256, 1152], P(('dp', 'mod'))
- grad_condition: float32 [64, 1152], P(('dp', 'mod'))
- grad_qkv: float32 [1152, 3456], P('dp')
- grad_proj: float32 [1152, 1152], P('dp')
- grad_gate: float32 [1152, 3072], P('dp')
- grad_up: float32 [1152, 3072], P('dp')
- grad_down: float32 [3072, 1152], P('dp')
- grad_mod: float32 [1152, 6912], P('dp', 'mod')
- grad_bias: float32 [6912], P('mod')
All inputs are finite; a program needn't handle non-finite values.
Results may differ from a plain program's by a relative error of at most 0.015.
Values may be sent and summed in bfloat16 or wider, within the bound.
A program may use at most 384 MiB of HBM per device.

v0:
```python
import math

import jax
import jax.numpy as jnp
from jax import lax
from jax.sharding import PartitionSpec as P

D = 1152
H = 16
HD = 72
GRID = 16
SEQ = 256
MICRO = 2


EPSILON = 1e-06


def norm_rows(field):
    scale_inv = lax.rsqrt(jnp.mean(field * field, axis=-1, keepdims=True) + EPSILON)
    return (field * scale_inv, scale_inv)


def norm_back(normed, scale_inv, gradient):
    return scale_inv * (gradient - normed * jnp.mean(gradient * normed, axis=-1, keepdims=True))


def embed_steps(timestep):
    half_width = D // 2
    frequency = jnp.exp(-math.log(10000.0) * jnp.arange(half_width, dtype=jnp.float32) / half_width)
    angles = timestep.astype(jnp.float32)[:, None] * frequency[None, :]
    return jnp.concatenate([jnp.cos(angles), jnp.sin(angles)], axis=1)


def rope_tables():
    quarter = HD // 4
    frequency = jnp.exp(-math.log(10000.0) * jnp.arange(quarter, dtype=jnp.float32) / quarter)
    position = jnp.arange(SEQ)
    row_index = (position // GRID).astype(jnp.float32)
    col_index = (position % GRID).astype(jnp.float32)
    angles = jnp.stack(
        [row_index[:, None] * frequency[None, :], col_index[:, None] * frequency[None, :]], axis=1
    )
    return (jnp.cos(angles), jnp.sin(angles))


def rotate(field, cosine_table, sine_table):
    leading = field.shape[:-1]
    quarters = field.reshape(leading + (2, 2, HD // 4))
    first_half = quarters[..., 0, :]
    second_half = quarters[..., 1, :]
    cosine_rows = cosine_table[:, None]
    sine_rows = sine_table[:, None]
    turned_first = first_half * cosine_rows - second_half * sine_rows
    turned_second = first_half * sine_rows + second_half * cosine_rows
    return jnp.stack([turned_first, turned_second], axis=-2).reshape(field.shape)


def pack_rows(arrays, count):
    return jnp.concatenate([array.reshape(count, -1) for array in arrays], axis=1).reshape(-1)


def unpack_rows(flat, shapes, count):
    pieces = []
    offset = 0
    for rows_all, columns in shapes:
        rows = rows_all // count
        pieces.append(flat[offset : offset + rows * columns].reshape(rows, columns))
        offset = offset + rows * columns
    return pieces


def layer_pass(block_in, mod_rows, cotangent, weights, tables):
    qkv_full, proj_full, gate_full, up_full, down_full = weights
    cosine_table, sine_table = tables
    images = block_in.shape[0]
    shift_first, scale_first, gate_first, shift_second, scale_second, gate_second = [
        mod_rows[:, None, number * D : (number + 1) * D] for number in range(6)
    ]
    heads_shape = (images, SEQ, H, HD)
    factor = 1.0 / math.sqrt(HD)
    inputs = block_in.astype(jnp.float32)
    normed_first, inv_first = norm_rows(inputs)
    entry_first = (normed_first * (1.0 + scale_first) + shift_first).astype(jnp.bfloat16)
    projected = jnp.einsum("bsd,de->bse", entry_first, qkv_full, preferred_element_type=jnp.float32)
    q_normed, q_inv = norm_rows(projected[..., :D].reshape(heads_shape))
    k_normed, k_inv = norm_rows(projected[..., D : 2 * D].reshape(heads_shape))
    queries = rotate(q_normed, cosine_table, sine_table).astype(jnp.bfloat16)
    keys_rot = rotate(k_normed, cosine_table, sine_table).astype(jnp.bfloat16)
    values = projected[..., 2 * D :].reshape(heads_shape).astype(jnp.bfloat16)
    scores = (
        jnp.einsum("bqhd,bkhd->bhqk", queries, keys_rot, preferred_element_type=jnp.float32)
        * factor
    )
    highest = jnp.max(scores, axis=-1, keepdims=True)
    log_total = highest + jnp.log(jnp.sum(jnp.exp(scores - highest), axis=-1, keepdims=True))
    weights_soft = jnp.exp(scores - log_total).astype(jnp.bfloat16)
    combined = (
        jnp.einsum("bhqk,bkhd->bqhd", weights_soft, values, preferred_element_type=jnp.float32)
        .reshape(images, SEQ, D)
        .astype(jnp.bfloat16)
    )
    attended = jnp.einsum("bsd,de->bse", combined, proj_full, preferred_element_type=jnp.float32)
    residual = inputs + gate_first * attended
    normed_second, inv_second = norm_rows(residual)
    entry_second = (normed_second * (1.0 + scale_second) + shift_second).astype(jnp.bfloat16)
    gate_proj = jnp.einsum(
        "bsd,df->bsf", entry_second, gate_full, preferred_element_type=jnp.float32
    )
    up_proj = jnp.einsum("bsd,df->bsf", entry_second, up_full, preferred_element_type=jnp.float32)
    sigma_gate = jax.nn.sigmoid(gate_proj)
    activated = gate_proj * sigma_gate
    hidden = (activated * up_proj).astype(jnp.bfloat16)
    branch = jnp.einsum("bsf,fd->bsd", hidden, down_full, preferred_element_type=jnp.float32)
    output = (residual + gate_second * branch).astype(jnp.bfloat16)
    grad_out = cotangent.astype(jnp.float32)
    d_gate_second = jnp.sum(grad_out * branch, axis=1)
    d_branch = (gate_second * grad_out).astype(jnp.bfloat16)
    d_hidden = jnp.einsum("bsd,fd->bsf", d_branch, down_full, preferred_element_type=jnp.float32)
    d_gate_proj = (d_hidden * up_proj * sigma_gate * (1.0 + gate_proj * (1.0 - sigma_gate))).astype(
        jnp.bfloat16
    )
    d_up_proj = (d_hidden * activated).astype(jnp.bfloat16)
    d_entry_second = jnp.einsum(
        "bsf,df->bsd", d_gate_proj, gate_full, preferred_element_type=jnp.float32
    )
    d_entry_second = d_entry_second + jnp.einsum(
        "bsf,df->bsd", d_up_proj, up_full, preferred_element_type=jnp.float32
    )
    d_shift_second = jnp.sum(d_entry_second, axis=1)
    d_scale_second = jnp.sum(d_entry_second * normed_second, axis=1)
    d_residual = grad_out + norm_back(
        normed_second, inv_second, d_entry_second * (1.0 + scale_second)
    )
    d_gate_first = jnp.sum(d_residual * attended, axis=1)
    d_attended = (gate_first * d_residual).astype(jnp.bfloat16)
    d_combined = (
        jnp.einsum("bse,de->bsd", d_attended, proj_full, preferred_element_type=jnp.float32)
        .astype(jnp.bfloat16)
        .reshape(heads_shape)
    )
    scores_again = (
        jnp.einsum("bqhd,bkhd->bhqk", queries, keys_rot, preferred_element_type=jnp.float32)
        * factor
    )
    recomputed = jnp.exp(scores_again - log_total)
    d_weights = jnp.einsum(
        "bqhd,bkhd->bhqk", d_combined, values, preferred_element_type=jnp.float32
    )
    d_scores = (
        recomputed * (d_weights - jnp.sum(recomputed * d_weights, axis=-1, keepdims=True))
    ).astype(jnp.bfloat16)
    d_values = jnp.einsum(
        "bhqk,bqhd->bkhd", weights_soft, d_combined, preferred_element_type=jnp.float32
    ).astype(jnp.bfloat16)
    d_queries = (
        (
            jnp.einsum("bhqk,bkhd->bqhd", d_scores, keys_rot, preferred_element_type=jnp.float32)
            * factor
        )
        .astype(jnp.bfloat16)
        .astype(jnp.float32)
    )
    d_keys = (
        (
            jnp.einsum("bhqk,bqhd->bkhd", d_scores, queries, preferred_element_type=jnp.float32)
            * factor
        )
        .astype(jnp.bfloat16)
        .astype(jnp.float32)
    )
    d_q_raw = norm_back(q_normed, q_inv, rotate(d_queries, cosine_table, -sine_table))
    d_k_raw = norm_back(k_normed, k_inv, rotate(d_keys, cosine_table, -sine_table))
    flat_shape = (images, SEQ, D)
    d_projected = jnp.concatenate(
        [
            d_q_raw.reshape(flat_shape),
            d_k_raw.reshape(flat_shape),
            d_values.astype(jnp.float32).reshape(flat_shape),
        ],
        axis=-1,
    ).astype(jnp.bfloat16)
    d_entry_first = jnp.einsum(
        "bse,de->bsd", d_projected, qkv_full, preferred_element_type=jnp.float32
    )
    d_shift_first = jnp.sum(d_entry_first, axis=1)
    d_scale_first = jnp.sum(d_entry_first * normed_first, axis=1)
    d_tokens = d_residual + norm_back(normed_first, inv_first, d_entry_first * (1.0 + scale_first))
    d_modulation = jnp.concatenate(
        [d_shift_first, d_scale_first, d_gate_first, d_shift_second, d_scale_second, d_gate_second],
        axis=1,
    ).astype(jnp.bfloat16)
    factors = (
        entry_first,
        d_projected,
        combined,
        d_attended,
        entry_second,
        d_gate_proj,
        d_up_proj,
        hidden,
        d_branch,
    )
    return (output, d_tokens, d_modulation, factors)


def body(
    tokens,
    condition,
    timestep,
    qkv_weight,
    out_weight,
    gate_weight,
    up_weight,
    down_weight,
    mod_weight,
    mod_bias,
    cotangent,
):
    gathered = (
        lax.all_gather(qkv_weight, "dp", axis=0, tiled=True),
        lax.all_gather(out_weight, "dp", axis=0, tiled=True),
        lax.all_gather(gate_weight, "dp", axis=0, tiled=True),
        lax.all_gather(up_weight, "dp", axis=0, tiled=True),
        lax.all_gather(down_weight, "dp", axis=0, tiled=True),
    )
    cond_total = condition.astype(jnp.float32) + embed_steps(timestep)
    acted_cond = jax.nn.silu(cond_total).astype(jnp.bfloat16)
    acted_group = lax.all_gather(acted_cond, "mod", axis=0, tiled=True)
    mod_part = (
        jnp.dot(acted_group, mod_weight, preferred_element_type=jnp.float32)
        + mod_bias.astype(jnp.float32)
    ).astype(jnp.bfloat16)
    modulation = lax.all_to_all(mod_part, "mod", split_axis=0, concat_axis=1, tiled=True).astype(
        jnp.float32
    )
    tables = rope_tables()
    per_micro = tokens.shape[0] // MICRO
    outputs = []
    token_grads = []
    mod_grads = []
    kept = []
    for micro_step in range(MICRO):
        start_row = micro_step * per_micro
        output, d_tokens, d_modulation, factors = layer_pass(
            tokens[start_row : start_row + per_micro],
            modulation[start_row : start_row + per_micro],
            cotangent[start_row : start_row + per_micro],
            gathered,
            tables,
        )
        outputs.append(output)
        token_grads.append(d_tokens)
        mod_grads.append(d_modulation)
        kept.append(factors)
    joined = [jnp.concatenate([factors[number] for factors in kept], axis=0) for number in range(9)]
    (
        entry_first,
        d_projected,
        combined,
        d_attended,
        entry_second,
        d_gate_proj,
        d_up_proj,
        hidden,
        d_branch,
    ) = joined
    grad_qkv = jnp.einsum(
        "bsd,bse->de", entry_first, d_projected, preferred_element_type=jnp.float32
    )
    grad_proj = jnp.einsum("bsd,bse->de", combined, d_attended, preferred_element_type=jnp.float32)
    grad_gate = jnp.einsum(
        "bsd,bsf->df", entry_second, d_gate_proj, preferred_element_type=jnp.float32
    )
    grad_up = jnp.einsum("bsd,bsf->df", entry_second, d_up_proj, preferred_element_type=jnp.float32)
    grad_down = jnp.einsum("bsf,bsd->fd", hidden, d_branch, preferred_element_type=jnp.float32)
    totals = (grad_qkv, grad_proj, grad_gate, grad_up, grad_down)
    output_tokens = jnp.concatenate(outputs, axis=0)
    grad_tokens = jnp.concatenate(token_grads, axis=0)
    mod_grad = jnp.concatenate(mod_grads, axis=0)
    mod_back = lax.all_to_all(mod_grad, "mod", split_axis=1, concat_axis=0, tiled=True)
    grad_mod_part = jnp.einsum(
        "id,ic->dc", acted_group, mod_back, preferred_element_type=jnp.float32
    )
    bias_part = jnp.sum(mod_back.astype(jnp.float32), axis=0)
    acted_grad_part = jnp.einsum(
        "ic,dc->id", mod_back, mod_weight, preferred_element_type=jnp.float32
    )
    acted_grad = lax.psum_scatter(
        acted_grad_part.astype(jnp.bfloat16), "mod", scatter_dimension=0, tiled=True
    ).astype(jnp.float32)
    sigma_cond = jax.nn.sigmoid(cond_total)
    grad_condition = acted_grad * sigma_cond * (1.0 + cond_total * (1.0 - sigma_cond))
    grad_bias = lax.psum(bias_part, "dp")
    count = lax.axis_size("dp")
    arrays = totals + (grad_mod_part,)
    shapes = [array.shape for array in arrays]
    flat = lax.psum_scatter(pack_rows(arrays, count), "dp", scatter_dimension=0, tiled=True)
    summed = unpack_rows(flat, shapes, count)
    finished = (
        lax.psum(summed[0].astype(jnp.bfloat16), "mod").astype(jnp.float32),
        lax.psum(summed[1].astype(jnp.bfloat16), "mod").astype(jnp.float32),
        lax.psum(summed[2].astype(jnp.bfloat16), "mod").astype(jnp.float32),
        lax.psum(summed[3].astype(jnp.bfloat16), "mod").astype(jnp.float32),
        lax.psum(summed[4].astype(jnp.bfloat16), "mod").astype(jnp.float32),
    )
    grad_mod = summed[5]
    return (
        output_tokens,
        grad_tokens,
        grad_condition,
        finished[0],
        finished[1],
        finished[2],
        finished[3],
        finished[4],
        grad_mod,
        grad_bias,
    )


def solution(mesh):
    in_specs = (
        P(("dp", "mod"), None, None),
        P(("dp", "mod"), None),
        P(("dp", "mod")),
        P("dp", None),
        P("dp", None),
        P("dp", None),
        P("dp", None),
        P("dp", None),
        P(None, "mod"),
        P("mod"),
        P(("dp", "mod"), None, None),
    )
    out_specs = (
        P(("dp", "mod"), None, None),
        P(("dp", "mod"), None, None),
        P(("dp", "mod"), None),
        P("dp", None),
        P("dp", None),
        P("dp", None),
        P("dp", None),
        P("dp", None),
        P("dp", "mod"),
        P("mod"),
    )
    return jax.shard_map(body, mesh=mesh, in_specs=in_specs, out_specs=out_specs, check_vma=False)
```

profile of v0, /device:TPU:0, one launch (start us, length us, event | category | flops | bytes accessed | tf_op | source)
XLA Modules:
  0.0 3114.9 jit_solution(3125690388604582008)
XLA Ops:
  10.8 6.2 all-gather
  30.2 102.3 %all-gather.7.cloned.1.call-done = bf16[1152,3456]{1,0:T(8,128)(2,1)} async-done(((bf16[144,3456]{1,0:T(8,128)(2,1)}), bf16[1152,3456]{1,0:T(8,128)(2,1)}) %all-gather.7.cloned.1.call-update) | async-done | bytes 7962640 | tf_op jit(solution)/shard_map/all_gather | solution.py:221
  141.2 5.8 convolution_bitcast_fusion.6
  192.0 6.7 subtract_convert_fusion.3
  226.5 71.0 %all-gather.11.cloned.1.call-done = bf16[1152,3072]{1,0:T(8,128)(2,1)} async-done(((bf16[144,3072]{1,0:T(8,128)(2,1)}), bf16[1152,3072]{1,0:T(8,128)(2,1)}) %all-gather.11.cloned.1.call-update) | async-done | bytes 7077904 | tf_op jit(solution)/shard_map/all_gather | solution.py:223
  297.5 7.0 fusion.111
  304.6 102.0 %all-gather.13.cloned.1.call-done = bf16[1152,3072]{1,0:T(8,128)(2,1)} async-done(((bf16[144,3072]{1,0:T(8,128)(2,1)}), bf16[1152,3072]{1,0:T(8,128)(2,1)}) %all-gather.13.cloned.1.call-update) | async-done | bytes 7077904 | tf_op jit(solution)/shard_map/all_gather | solution.py:224
  406.6 7.1 fusion.109
  413.6 102.0 %all-gather.15.cloned.1.call-done = bf16[3072,1152]{1,0:T(8,128)(2,1)} async-done(((bf16[384,1152]{1,0:T(8,128)(2,1)}), bf16[3072,1152]{1,0:T(8,128)(2,1)}) %all-gather.15.cloned.1.call-update) | async-done | bytes 7077904 | tf_op jit(solution)/shard_map/all_gather | solution.py:225
  515.6 9.1 multiply_convert_fusion.2
  524.8 6.4 fusion.165
  543.8 6.7 multiply_convert_fusion.4
  555.3 6.3 fusion.164
  567.1 6.7 fusion.78
  669.4 6.3 fusion.161
  692.2 11.4 convolution_bitcast_fusion
  703.7 13.4 reshape.1577
  717.0 11.6 constant_dynamic-update-slice_fusion.17
  738.5 8.6 convolution_bitcast_fusion.3
  747.0 12.7 reshape.1579
  759.8 8.6 convolution_bitcast_fusion.2
  768.4 12.8 reshape.1580
  781.2 9.8 convolution_bitcast_fusion.1
  791.0 12.6 reshape.1581
  808.4 12.5 constant_dynamic-update-slice_fusion.15
  820.9 7.2 constant_dynamic-update-slice_fusion.14
  841.0 10.6 reshape.1582
  857.3 48.5 %copy.290 = f32[1,17496,8,128]{3,1,2,0:T(8,128)} copy(f32[1,17496,8,128]{3,2,1,0:T(8,128)} %bitcast.118) | data formatting | bytes 143327232
  911.2 2091.2 %all-reduce.6.cloned.1.call-done = f32[17915904]{0:T(1024)} async-done(((f32[17915904]{0:T(1024)}), f32[17915904]{0:T(1024)}) %all-reduce.6.cloned.1.call-update) | async-done | bytes 71663632
  3023.0 19.5 psum.47
  3045.3 12.0 all-reduce
  3060.9 38.5 %all-reduce.8.cloned.1.call-done = (bf16[144,3456]{1,0:T(8,128)(2,1)}, bf16[144,1152]{1,0:T(8,128)(2,1)}, bf16[144,3072]{1,0:T(8,128)(2,1)}, bf16[144,3072]{1,0:T(8,128)(2,1)}, bf16[384,1152]{1,0:T(8,128)(2,1)}) async-done(((bf16[144,3456]{1,0:T(8,128)(2,1)}, bf16[144,1152]{1,0:T(8,128)(2,1)}, bf16[144,3072]{1,0:T(8,128)(2,1)}, bf16[144,3072]{1,0:T(8,128)(2,1)}, bf16[384,1152]{1,0:T(8,128)(2,1)}), ...) | async-done | bytes 3981328 | tf_op jit(solution)/shard_map/psum | solution.py:301
  (571 shorter events, 303.9 us)
Async XLA Ops:
  7.2 125.3 %all-gather.7.cloned.1.call-start = ((), (), s32[]{:S(2)}) async-start(), calls=%async_computation.2 | async-start | bytes 8957952 | tf_op jit(solution)/shard_map/all_gather | solution.py:221
  7.9 208.0 %all-gather.9.cloned.1.call-start = ((), (), s32[]{:S(2)}) async-start(), calls=%async_computation.3 | async-start | bytes 2985984 | tf_op jit(solution)/shard_map/all_gather | solution.py:222
  8.7 288.8 %all-gather.11.cloned.1.call-start = ((), (), s32[]{:S(2)}) async-start(), calls=%async_computation.4 | async-start | bytes 7962624 | tf_op jit(solution)/shard_map/all_gather | solution.py:223
  9.4 397.2 %all-gather.13.cloned.1.call-start = ((), (), s32[]{:S(2)}) async-start(), calls=%async_computation.5 | async-start | bytes 7962624 | tf_op jit(solution)/shard_map/all_gather | solution.py:224
  21.1 7.2 all-to-all-start
  24.4 491.3 %all-gather.15.cloned.1.call-start = ((), (), s32[]{:S(2)}) async-start(), calls=%async_computation.6 | async-start | bytes 7962624 | tf_op jit(solution)/shard_map/all_gather | solution.py:225
  30.2 102.3 %copy-start.86 = (bf16[1,256,1152]{2,1,0:T(8,128)(2,1)}, bf16[1,256,1152]{2,1,0:T(8,128)(2,1)S(1)}, u32[]{:S(2)}) copy-start(bf16[1,256,1152]{2,1,0:T(8,128)(2,1)S(1)} %get-tuple-element.115) | copy-start | bytes 1769476
  30.2 110.9 %copy-start.84 = (bf16[1,256,1152]{2,1,0:T(8,128)(2,1)}, bf16[1,256,1152]{2,1,0:T(8,128)(2,1)S(1)}, u32[]{:S(2)}) copy-start(bf16[1,256,1152]{2,1,0:T(8,128)(2,1)S(1)} %get-tuple-element.114) | copy-start | bytes 1769476
  153.6 34.1 %copy-start.16 = (f32[1,256,1152]{1,0,2:T(1,128)}, f32[1,256,1152]{1,0,2:T(1,128)S(1)}, u32[]{:S(2)}) copy-start(f32[1,256,1152]{1,0,2:T(1,128)S(1)} %copy.200) | copy-start | bytes 3538948
  158.4 30.2 copy-start.14
  204.2 14.8 copy-start.33
  665.0 11.9 slice-start.10
  686.3 149.3 %all-to-all-start.1 = ((bf16[2,4,1728]{2,0,1:T(2,128)(2,1)}), bf16[2,4,1728]{2,0,1:T(2,128)(2,1)}, u32[]{:S(2)}, u32[]{:S(2)}) async-start(bf16[2,4,1728]{2,0,1:T(2,128)(2,1)} %copy.261), calls=%async_computation.1 | async-start | bytes 57344 | tf_op jit(solution)/shard_map/all_to_all | solution.py:281
  690.2 2312.2 %all-reduce.6.cloned.1.call-start = ((), (), s32[]{:S(2)}) async-start(), calls=%async_computation.7 | async-start | bytes 143327232
  717.0 11.7 copy-start.81
  717.0 11.7 copy-start.89
  747.0 12.7 copy-start.27
  768.4 12.8 copy-start.58
  768.4 12.8 copy-start.76
  768.4 12.8 copy-start.77
  803.6 17.3 slice-start
  803.6 17.3 slice-start.1
  808.3 12.5 slice-start.2
  808.3 12.5 slice-start.3
  808.3 19.7 slice-start.4
  808.3 19.7 slice-start.5
  808.4 21.7 slice-start.6
  905.8 2193.6 %all-reduce.8.cloned.1.call-start = ((), (), s32[]{:S(2)}) async-start(), calls=%async_computation.8 | async-start | bytes 7962624 | tf_op jit(solution)/shard_map/psum | solution.py:301
  3020.6 21.9 copy-start.111
  3042.5 14.9 copy-start.136
  3042.5 14.9 copy-start.138
  3042.5 14.9 copy-start.142
  (155 other events, 578.2 us)
Sparse Core Ops, SparseCore 0:
  10.2 122.2 all-gather.6
  134.7 53.1 all-gather.8
  190.1 107.3 all-gather.10
  299.6 106.9 all-gather.12
  408.6 106.9 all-gather.14
  906.0 2096.4 all-reduce.5
  3016.5 82.8 all-reduce.7
where the time goes:
time: 3120 us; the launch traced here: 3110 us
  waiting for transfers between devices  2510 us (80%)
  local copies, waits for them, and re-layouts  280 us (9%)
  matrix products  173 us (6%)
  other arithmetic  86.7 us (3%)
  blocking collectives  37.7 us (1%)
    unnamed x8, waiting for transfers between devices  2090 us
    unnamed x376, local copies, waits for them, and re-layouts  122 us
    all_gather x1, waiting for transfers between devices, body(): lax.all_gather(qkv_weight, 'dp', axis=0, tiled=True)  102 us
    all_gather x1, waiting for transfers between devices, body(): lax.all_gather(up_weight, 'dp', axis=0, tiled=True)  102 us
    all_gather x1, waiting for transfers between devices, body(): lax.all_gather(down_weight, 'dp', axis=0, tiled=True)  102 us
    all_gather x1, waiting for transfers between devices, body(): lax.all_gather(gate_weight, 'dp', axis=0, tiled=True)  71 us
    reshape x6, local copies, waits for them, and re-layouts, pack_rows(): array.reshape(count, -1)  67.8 us
  transfers between devices with their start and end apart: 9, of which 7 were waited for; matrix products, arithmetic and copies ran while one was open for 8% of the time, Pallas kernels for 0%

commit v1 on v0

--- a/solution.py
+++ b/solution.py
@@ -3,6 +3,8 @@
 import jax
 import jax.numpy as jnp
 from jax import lax
+from jax.experimental import pallas as pl
+from jax.experimental.pallas import tpu as pltpu
 from jax.sharding import PartitionSpec as P
 
 D = 1152
@@ -204,7 +206,428 @@
     return (output, d_tokens, d_modulation, factors)
 
 
-def body(
+MESH = pl.DeviceIdType.MESH
+WIDTH = 384
+LANE_HALF = 2304
+FF_HALF = 1536
+BF16 = jnp.bfloat16
+F32 = jnp.float32
+
+
+def place():
+    dp = lax.axis_index("dp")
+    mod = lax.axis_index("mod")
+    return dp // 2, dp % 2, mod // 2, mod % 2
+
+
+def device(z, x, y, c):
+    return (z * 2 + x, y * 2 + c)
+
+
+def greet(peers):
+    barrier = pltpu.get_barrier_semaphore()
+    for peer in peers:
+        pl.semaphore_signal(barrier, inc=1, device_id=peer, device_id_type=MESH)
+    pl.semaphore_wait(barrier, len(peers))
+
+
+def neighbours(z, x, y, c):
+    around = [device((z + step) % 4, x, y, c) for step in (1, 2, 3)]
+    return around + [device(z, 1 - x, y, c), device(z, x, 1 - y, c), device(z, x, y, 1 - c)]
+
+
+def send(source, target, send_sem, recv_sem, peer):
+    pltpu.make_async_remote_copy(
+        src_ref=source,
+        dst_ref=target,
+        send_sem=send_sem,
+        recv_sem=recv_sem,
+        device_id=peer,
+        device_id_type=MESH,
+    ).start()
+
+
+def drain(window, sem):
+    pltpu.make_async_copy(window, window, sem).wait()
+
+
+class Piece:
+    def __init__(self, source, target, row, rows, column, edge):
+        self.source, self.target = source, target
+        self.row, self.rows, self.column, self.edge = row, rows, column, edge
+
+
+def gather_pieces(refs, c, edge_of):
+    packed, gate, up, down, packed_all, gate_all, up_all, down_all = refs
+    pieces = []
+    for j in range(6):
+        pieces.append(Piece(packed, packed_all, 0, 144, c * LANE_HALF + j * WIDTH, edge_of(144, j)))
+    for j in range(4):
+        pieces.append(Piece(gate, gate_all, 0, 144, c * FF_HALF + j * WIDTH, edge_of(144, j)))
+        pieces.append(Piece(up, up_all, 0, 144, c * FF_HALF + j * WIDTH, edge_of(144, j)))
+    for j in range(3):
+        pieces.append(Piece(down, down_all, c * 192, 192, j * WIDTH, edge_of(192, j)))
+    return pieces
+
+
+class Gather:
+    def __init__(self, refs, sems, spot):
+        self.z, self.x, self.y, self.c = spot
+        self.pieces = gather_pieces(refs, self.c, lambda rows, j: rows // 3)
+        self.send_sems, self.recv_sems, self.own_sems = sems
+        self.refs = refs
+
+    def columns(self, piece):
+        return pl.ds(pl.multiple_of(piece.column, 128), WIDTH)
+
+    def part(self, piece):
+        keep = piece.rows - piece.edge
+        return pl.ds(pl.multiple_of(piece.row + self.y * piece.edge, 16), keep), keep
+
+    def mine(self, piece):
+        return pl.ds(pl.multiple_of(piece.row + self.y * (piece.rows - piece.edge), 16), piece.edge)
+
+    def own_copies(self):
+        for k in range(4):
+            pltpu.make_async_copy(
+                self.refs[k], self.refs[4 + k].at[self.z, self.x], self.own_sems.at[k]
+            ).start()
+
+    def own_done(self):
+        for k in range(4):
+            drain(self.refs[k], self.own_sems.at[k])
+
+    def start_z(self, t):
+        p = self.pieces[t]
+        rows, _ = self.part(p)
+        here = p.source.at[rows, self.columns(p)]
+        there = p.target.at[self.z, self.x, rows, self.columns(p)]
+        for step in (1, 3, 2):
+            peer = device((self.z + step) % 4, self.x, self.y, self.c)
+            send(here, there, self.send_sems.at[0, t], self.recv_sems.at[0, t], peer)
+        peer = device(self.z, 1 - self.x, self.y, self.c)
+        send(here, there, self.send_sems.at[1, t], self.recv_sems.at[1, t], peer)
+
+    def start_x(self, t):
+        p = self.pieces[t]
+        rows, keep = self.part(p)
+        columns = self.columns(p)
+        drain(p.target.at[pl.ds(0, 3), 0, pl.ds(0, keep), pl.ds(0, WIDTH)], self.recv_sems.at[0, t])
+        x_peer = device(self.z, 1 - self.x, self.y, self.c)
+        y_peer = device(self.z, self.x, 1 - self.y, self.c)
+        for step in (1, 3, 2):
+            other = (self.z + step) % 4
+            block = p.target.at[other, self.x, rows, columns]
+            send(block, block, self.send_sems.at[1, t], self.recv_sems.at[1, t], x_peer)
+        for step in (1, 3, 2):
+            other = (self.z + step) % 4
+            block = p.target.at[other, self.x, self.mine(p), columns]
+            send(block, block, self.send_sems.at[2, t], self.recv_sems.at[2, t], y_peer)
+
+    def start_y(self, t):
+        p = self.pieces[t]
+        _, keep = self.part(p)
+        columns = self.columns(p)
+        drain(p.target.at[:, 0, pl.ds(0, keep), pl.ds(0, WIDTH)], self.recv_sems.at[1, t])
+        y_peer = device(self.z, self.x, 1 - self.y, self.c)
+        block = p.target.at[:, 1 - self.x, self.mine(p), columns]
+        send(block, block, self.send_sems.at[2, t], self.recv_sems.at[2, t], y_peer)
+
+    def start_c(self, t):
+        p = self.pieces[t]
+        columns = self.columns(p)
+        half = pl.ds(pl.multiple_of(p.row, 16), p.rows)
+        self.drain_seven(p.edge, self.recv_sems.at[2, t])
+        peer = device(self.z, self.x, self.y, 1 - self.c)
+        block = p.target.at[:, 1 - self.x, half, columns]
+        send(block, block, self.send_sems.at[3, t], self.recv_sems.at[3, t], peer)
+        for step in (1, 2, 3):
+            block = p.target.at[(self.z + step) % 4, self.x, half, columns]
+            send(block, block, self.send_sems.at[3, t], self.recv_sems.at[3, t], peer)
+
+    def arrived(self, t):
+        self.drain_seven(self.pieces[t].rows, self.recv_sems.at[3, t])
+
+    def drain_seven(self, rows, sem):
+        high = 96 if rows > 144 else rows
+        drain(self.refs[4].at[pl.ds(0, rows // high), 0, pl.ds(0, high), pl.ds(0, 7 * WIDTH)], sem)
+
+    def sent_z(self, t):
+        p = self.pieces[t]
+        _, keep = self.part(p)
+        drain(p.target.at[pl.ds(0, 3), 0, pl.ds(0, keep), pl.ds(0, WIDTH)], self.send_sems.at[0, t])
+
+    def sent_rest(self, t):
+        p = self.pieces[t]
+        _, keep = self.part(p)
+        drain(p.target.at[:, 0, pl.ds(0, keep), pl.ds(0, WIDTH)], self.send_sems.at[1, t])
+        for stage, rows in ((2, p.edge), (3, p.rows)):
+            self.drain_seven(rows, self.send_sems.at[stage, t])
+
+
+N_PIECES = 17
+
+
+def gather_kernel(*refs):
+    arrays, sems = refs[:8], refs[8:]
+    spot = place()
+    greet(neighbours(*spot))
+    gather = Gather(arrays, sems, spot)
+    gather.own_copies()
+    ahead = 2
+    for t in range(N_PIECES + 4 + ahead):
+        if t < N_PIECES:
+            if t >= ahead:
+                gather.sent_z(t - ahead)
+            gather.start_z(t)
+        if 0 <= t - ahead < N_PIECES:
+            gather.start_x(t - ahead)
+        if 0 <= t - ahead - 1 < N_PIECES:
+            gather.start_y(t - ahead - 1)
+        if 0 <= t - ahead - 2 < N_PIECES:
+            gather.start_c(t - ahead - 2)
+        if 0 <= t - ahead - 3 < N_PIECES:
+            gather.arrived(t - ahead - 3)
+    for t in range(N_PIECES - ahead, N_PIECES):
+        gather.sent_z(t)
+    for t in range(N_PIECES):
+        gather.sent_rest(t)
+    gather.own_done()
+
+
+def gather_weights(packed, gate, up, down):
+    hbm = pl.BlockSpec(memory_space=pl.ANY)
+    shapes = [
+        jax.ShapeDtypeStruct((4, 2) + array.shape, BF16) for array in (packed, gate, up, down)
+    ]
+    return pl.pallas_call(
+        gather_kernel,
+        out_shape=shapes,
+        in_specs=[hbm] * 4,
+        out_specs=[hbm] * 4,
+        scratch_shapes=[
+            pltpu.SemaphoreType.DMA((4, N_PIECES)),
+            pltpu.SemaphoreType.DMA((4, N_PIECES)),
+            pltpu.SemaphoreType.DMA((4,)),
+        ],
+        name="gather_weights",
+        compiler_params=pltpu.CompilerParams(
+            collective_id=0, has_side_effects=True, vmem_limit_bytes=16 << 20
+        ),
+    )(packed, gate, up, down)
+
+
+SCATTER_ROWS = (144,) * 14 + (192,) * 3
+SCATTER_EDGE = tuple((32, 48)[j % 2] for j in range(14)) + (48,) * 3
+
+
+class Scatter:
+    def __init__(self, bufs, sems, outs, spot):
+        self.z, self.x, self.y, self.c = spot
+        self.held, self.got_y, self.got_x, self.got_z, self.mid, self.got_f, self.fin, self.got_c = bufs
+        self.send_sems, self.recv_sems = sems
+        self.outs = outs
+
+    def shape(self, t):
+        return SCATTER_ROWS[t], SCATTER_EDGE[t]
+
+    def part(self, t):
+        rows, edge = self.shape(t)
+        return pl.ds(pl.multiple_of(self.y * edge, 16), rows - edge)
+
+    def buf(self, group, t, rows=None):
+        big, small = group
+        return small.at[t] if t < 14 else big.at[t - 14]
+
+    def start_y(self, t):
+        rows, edge = self.shape(t)
+        theirs = pl.ds(pl.multiple_of((1 - self.y) * (rows - edge), 16), edge)
+        peer = device(self.z, self.x, 1 - self.y, self.c)
+        send(
+            self.buf(self.held, t).at[:, :, theirs, :],
+            self.buf(self.got_y, t).at[:, :, pl.ds(0, edge), :],
+            self.send_sems.at[0, t],
+            self.recv_sems.at[0, t],
+            peer,
+        )
+
+    def start_x(self, t):
+        rows, edge = self.shape(t)
+        held = self.buf(self.held, t)
+        got = self.buf(self.got_y, t)
+        drain(got.at[:, :, pl.ds(0, edge), :], self.recv_sems.at[0, t])
+        mine = pl.ds(pl.multiple_of(self.y * (rows - edge), 16), edge)
+
+        for k in range(4):
+            for x in range(2):
+                total = held[k, x, mine, :].astype(F32) + got[k, x, :edge, :].astype(F32)
+                held[k, x, mine, :] = total.astype(BF16)
+        peer = device(self.z, 1 - self.x, self.y, self.c)
+        send(
+            held.at[:, 1 - self.x, self.part(t), :],
+            self.buf(self.got_x, t).at[:, pl.ds(0, rows - edge), :],
+            self.send_sems.at[1, t],
+            self.recv_sems.at[1, t],
+            peer,
+        )
+
+    def start_z(self, t):
+        rows, edge = self.shape(t)
+        held = self.buf(self.held, t)
+        got = self.buf(self.got_x, t)
+        drain(got.at[:, pl.ds(0, rows - edge), :], self.recv_sems.at[1, t])
+        part = self.part(t)
+        for k in range(4):
+            total = held[k, self.x, part, :].astype(F32) + got[k, : rows - edge, :].astype(F32)
+            held[k, self.x, part, :] = total.astype(BF16)
+        for step in (1, 3, 2):
+            other = (self.z + step) % 4
+            send(
+                held.at[other, self.x, part, :],
+                self.buf(self.got_z, t).at[step - 1, pl.ds(0, rows - edge), :],
+                self.send_sems.at[2, t],
+                self.recv_sems.at[2, t],
+                device(other, self.x, self.y, self.c),
+            )
+
+    def start_f(self, t):
+        rows, edge = self.shape(t)
+        held = self.buf(self.held, t)
+        got = self.buf(self.got_z, t)
+        drain(got.at[:, pl.ds(0, rows - edge), :], self.recv_sems.at[2, t])
+        total = held[self.z, self.x, self.part(t), :].astype(F32)
+        for k in range(3):
+            total = total + got[k, : rows - edge, :].astype(F32)
+        mid = self.buf(self.mid, t)
+        mid[: rows - edge, :] = total.astype(BF16)
+        send(
+            mid.at[pl.ds(0, rows - edge), :],
+            self.buf(self.got_f, t).at[pl.ds(0, rows - edge), :],
+            self.send_sems.at[3, t],
+            self.recv_sems.at[3, t],
+            device(self.z, self.x, 1 - self.y, self.c),
+        )
+
+    def start_c(self, t):
+        rows, edge = self.shape(t)
+        mid, got, fin = self.buf(self.mid, t), self.buf(self.got_f, t), self.buf(self.fin, t)
+        y = self.y
+        drain(got.at[pl.ds(0, rows - edge), :], self.recv_sems.at[3, t])
+        both = rows - 2 * edge
+
+        def at(offset, count):
+            return pl.ds(pl.multiple_of(offset, 16), count)
+
+        fin[at(y * (rows - edge), edge), :] = mid[at(y * both, edge), :]
+        fin[at((1 - y) * (rows - edge), edge), :] = got[at((1 - y) * both, edge), :]
+        total = mid[at((1 - y) * edge, both), :].astype(F32) + got[at(y * edge, both), :].astype(F32)
+        fin[edge : edge + both, :] = total.astype(BF16)
+        send(
+            fin,
+            self.buf(self.got_c, t),
+            self.send_sems.at[4, t],
+            self.recv_sems.at[4, t],
+            device(self.z, self.x, self.y, 1 - self.c),
+        )
+        self.store(t, fin, self.c)
+
+    def finish(self, t):
+        got = self.buf(self.got_c, t)
+        drain(got, self.recv_sems.at[4, t])
+        self.store(t, got, 1 - self.c)
+
+    def store(self, t, block, core):
+        packed, gate, up, down = self.outs
+        if t < 6:
+            columns = pl.ds(pl.multiple_of(core * LANE_HALF + t * WIDTH, 128), WIDTH)
+            packed[:, columns] = block[...].astype(F32)
+        elif t < 14:
+            target = (gate, up)[(t - 6) % 2]
+            columns = pl.ds(pl.multiple_of(core * FF_HALF + (t - 6) // 2 * WIDTH, 128), WIDTH)
+            target[:, columns] = block[...].astype(F32)
+        else:
+            rows = pl.ds(pl.multiple_of(core * 192, 16), 192)
+            down[rows, (t - 14) * WIDTH : (t - 13) * WIDTH] = block[...].astype(F32)
+
+    def sent(self, t):
+        rows, edge = self.shape(t)
+        drain(self.buf(self.got_y, t).at[:, :, pl.ds(0, edge), :], self.send_sems.at[0, t])
+        drain(self.buf(self.got_x, t).at[:, pl.ds(0, rows - edge), :], self.send_sems.at[1, t])
+        drain(self.buf(self.got_z, t).at[:, pl.ds(0, rows - edge), :], self.send_sems.at[2, t])
+        drain(self.buf(self.got_f, t).at[pl.ds(0, rows - edge), :], self.send_sems.at[3, t])
+        drain(self.buf(self.got_c, t), self.send_sems.at[4, t])
+
+
+def scatter_scratch():
+    shapes = []
+    for lead, share in (((4, 2), 1), ((4, 2), 3), ((4,), 2), ((3,), 2), ((), 2), ((), 2), ((), 1), ((), 1)):
+        for count, rows, edges in ((3, 192, (48, 48)), (14, 144, (32, 48))):
+            height = {1: rows, 3: max(edges), 2: rows - min(edges)}[share]
+            shapes.append(pltpu.VMEM((count,) + lead + (height, WIDTH), BF16))
+    return shapes
+
+
+def scatter_kernel(half_packed, half_gate, half_up, half_down, *rest):
+    outs = rest[:4]
+    scratch = rest[4:20]
+    send_sems, recv_sems, load_sems = rest[20:]
+    bufs = [(scratch[2 * k], scratch[2 * k + 1]) for k in range(8)]
+    spot = place()
+    greet(neighbours(*spot))
+    scatter = Scatter(bufs, (send_sems, recv_sems), outs, spot)
+    order = list(range(14, 17)) + list(range(6, 14)) + list(range(6))
+    loads = []
+    for t in range(N_PIECES):
+        if t < 6:
+            source = half_packed.at[:, :, :, pl.ds(t * WIDTH, WIDTH)]
+        elif t < 14:
+            source = (half_gate, half_up)[(t - 6) % 2].at[:, :, :, pl.ds((t - 6) // 2 * WIDTH, WIDTH)]
+        else:
+            source = half_down.at[:, :, :, pl.ds((t - 14) * WIDTH, WIDTH)]
+        loads.append(pltpu.make_async_copy(source, scatter.buf(scatter.held, t), load_sems.at[t]))
+    for t in order:
+        loads[t].start()
+    ahead = 2
+    for k in range(N_PIECES + 6 + ahead):
+        if k < N_PIECES:
+            loads[order[k]].wait()
+            scatter.start_y(order[k])
+        for lag, stage in enumerate(
+            (scatter.start_x, scatter.start_z, scatter.start_f, scatter.start_c, scatter.finish)
+        ):
+            if 0 <= k - ahead - lag < N_PIECES:
+                stage(order[k - ahead - lag])
+    for t in range(N_PIECES):
+        scatter.sent(t)
+
+
+def scatter_grads(half_packed, half_gate, half_up, half_down):
+    hbm = pl.BlockSpec(memory_space=pl.ANY)
+    vmem = pl.BlockSpec(memory_space=pltpu.VMEM)
+    return pl.pallas_call(
+        scatter_kernel,
+        out_shape=[
+            jax.ShapeDtypeStruct((144, 4608), F32),
+            jax.ShapeDtypeStruct((144, 3072), F32),
+            jax.ShapeDtypeStruct((144, 3072), F32),
+            jax.ShapeDtypeStruct((384, 1152), F32),
+        ],
+        in_specs=[hbm] * 4,
+        out_specs=[vmem] * 4,
+        scratch_shapes=scatter_scratch()
+        + [
+            pltpu.SemaphoreType.DMA((5, N_PIECES)),
+            pltpu.SemaphoreType.DMA((5, N_PIECES)),
+            pltpu.SemaphoreType.DMA((N_PIECES,)),
+        ],
+        name="scatter_grads",
+        compiler_params=pltpu.CompilerParams(
+            collective_id=1, has_side_effects=True, vmem_limit_bytes=60 << 20
+        ),
+    )(half_packed, half_gate, half_up, half_down)
+
+
+def body_general(
     tokens,
     condition,
     timestep,
@@ -319,6 +742,133 @@
     )
 
 
+def pair_exchange(array):
+    return lax.ppermute(array, "mod", [(0, 1), (1, 0), (2, 3), (3, 2)])
+
+
+def body_fast(
+    tokens,
+    condition,
+    timestep,
+    qkv_weight,
+    out_weight,
+    gate_weight,
+    up_weight,
+    down_weight,
+    mod_weight,
+    mod_bias,
+    cotangent,
+):
+    core = lax.axis_index("mod") % 2
+    packed = jnp.concatenate([qkv_weight, out_weight], axis=1)
+    packed_all, gate_all, up_all, down_all = gather_weights(
+        packed, gate_weight, up_weight, down_weight
+    )
+    packed_all = packed_all.reshape(D, 4 * D)
+    gathered = (
+        packed_all[:, : 3 * D],
+        packed_all[:, 3 * D :],
+        gate_all.reshape(D, -1),
+        up_all.reshape(D, -1),
+        down_all.reshape(-1, D),
+    )
+    cond_total = condition.astype(jnp.float32) + embed_steps(timestep)
+    acted_cond = jax.nn.silu(cond_total).astype(jnp.bfloat16)
+    acted_group = lax.all_gather(acted_cond, "mod", axis=0, tiled=True)
+    mod_part = (
+        jnp.dot(acted_group, mod_weight, preferred_element_type=jnp.float32)
+        + mod_bias.astype(jnp.float32)
+    ).astype(jnp.bfloat16)
+    modulation = lax.all_to_all(mod_part, "mod", split_axis=0, concat_axis=1, tiled=True).astype(
+        jnp.float32
+    )
+    tables = rope_tables()
+    output_tokens, grad_tokens, mod_grad, factors = layer_pass(
+        tokens, modulation, cotangent, gathered, tables
+    )
+    (
+        entry_first,
+        d_projected,
+        combined,
+        d_attended,
+        entry_second,
+        d_gate_proj,
+        d_up_proj,
+        hidden,
+        d_branch,
+    ) = [factor.reshape(-1, factor.shape[-1]) for factor in factors]
+
+    def pair(factor):
+        return jnp.concatenate([factor, pair_exchange(factor)], axis=0)
+
+    def half(factor, width):
+        return lax.dynamic_slice_in_dim(factor, core * width, width, 1)
+
+    def other(factor, width):
+        return lax.dynamic_slice_in_dim(factor, (1 - core) * width, width, 1)
+
+    def pair_half(factor, width):
+        return jnp.concatenate(
+            [half(factor, width), pair_exchange(other(factor, width))], axis=0
+        )
+
+    def outer(left, right):
+        return lax.dot_general(
+            left, right, (((0,), (0,)), ((), ())), preferred_element_type=jnp.float32
+        ).astype(BF16)
+
+    entry_pair = pair(entry_first)
+    second_pair = jnp.where(core == 0, entry_pair, pair(combined))
+    packed_pair = pair_half(jnp.concatenate([d_projected, d_attended], axis=1), LANE_HALF)
+    half_packed = jnp.concatenate(
+        [outer(entry_pair, packed_pair[:, :D]), outer(second_pair, packed_pair[:, D:])], axis=1
+    )
+    entry_pair_b = pair(entry_second)
+    half_gate = outer(entry_pair_b, pair_half(d_gate_proj, FF_HALF))
+    half_up = outer(entry_pair_b, pair_half(d_up_proj, FF_HALF))
+    by_core = hidden.reshape(-1, 8, 2, 192).transpose(0, 2, 1, 3).reshape(-1, 2 * FF_HALF)
+    half_down = outer(pair_half(by_core, FF_HALF), pair(d_branch))
+    grads = scatter_grads(
+        half_packed.reshape(4, 2, 144, -1),
+        half_gate.reshape(4, 2, 144, -1),
+        half_up.reshape(4, 2, 144, -1),
+        half_down.reshape(4, 2, 192, -1),
+    )
+    mod_back = lax.all_to_all(mod_grad, "mod", split_axis=1, concat_axis=0, tiled=True)
+    acted_all = lax.all_gather(acted_group, "dp", axis=0, tiled=True)
+    back_all = lax.all_gather(mod_back, "dp", axis=0, tiled=True)
+    rows = D // 8
+    acted_rows = lax.dynamic_slice_in_dim(acted_all, lax.axis_index("dp") * rows, rows, 1)
+    grad_mod = jnp.einsum("id,ic->dc", acted_rows, back_all, preferred_element_type=jnp.float32)
+    grad_bias = jnp.sum(back_all.astype(jnp.float32), axis=0)
+    acted_grad_part = jnp.einsum(
+        "ic,dc->id", mod_back, mod_weight, preferred_element_type=jnp.float32
+    )
+    acted_grad = lax.psum_scatter(
+        acted_grad_part.astype(jnp.bfloat16), "mod", scatter_dimension=0, tiled=True
+    ).astype(jnp.float32)
+    sigma_cond = jax.nn.sigmoid(cond_total)
+    grad_condition = acted_grad * sigma_cond * (1.0 + cond_total * (1.0 - sigma_cond))
+    return (
+        output_tokens,
+        grad_tokens,
+        grad_condition,
+        grads[0][:, : 3 * D],
+        grads[0][:, 3 * D :],
+        grads[1],
+        grads[2],
+        grads[3],
+        grad_mod,
+        grad_bias,
+    )
+
+
+def pick_body(mesh):
+    if dict(mesh.shape) == {"dp": 8, "mod": 4}:
+        return body_fast
+    return body_general
+
+
 def solution(mesh):
     in_specs = (
         P(("dp", "mod"), None, None),
@@ -345,4 +895,4 @@
         P("dp", "mod"),
         P("mod"),
     )
-    return jax.shard_map(body, mesh=mesh, in_specs=in_specs, out_specs=out_specs, check_vma=False)
+    return jax.shard_map(pick_body(mesh), mesh=mesh, in_specs=in_specs, out_specs=out_specs, check_vma=False)

time: 3120 us -> 750 us (0.24)
  waiting for transfers between devices: 2510 us -> 0.03 us
  Pallas kernels: 0 us -> 293 us
  local copies, waits for them, and re-layouts: 280 us -> 143 us
  blocking collectives: 37.7 us -> 80.8 us
    unnamed x8 -> x0, waiting for transfers between devices: 2090 us -> none
    all_gather x5 -> x0, waiting for transfers between devices: 377 us -> none  [the longest x1 102 us: body(): lax.all_gather(qkv_weight, 'dp', axis=0, tiled=True)]
    pallas_call x0 -> x2, Pallas kernels: none -> 293 us  [the longest x1 156 us: scatter_grads(): pl.pallas_call(scatter_kernel, out_shape=[jax.ShapeDtypeStruct((144, 4608...]
    unnamed x376 -> x176, local copies, waits for them, and re-layouts: 122 us -> 38.4 us
    reshape x7 -> x3, local copies, waits for them, and re-layouts: 69.1 us -> 4.41 us  [the longest x2 3.01 us: body_fast(): factor.reshape(-1, factor.shape[-1])]
    all_gather x1 -> x3, blocking collectives: 6.21 us -> 70.3 us  [the longest x1 33.3 us: body_fast(): acted_all = lax.all_gather(acted_group, 'dp', axis=0, tiled=True)]
    psum x1 -> x0, waiting for transfers between devices: 38.5 us -> none  [body(): lax.psum(summed[0].astype(jnp.bfloat16), 'mod').astype(jnp.float32)]
  transfers between devices with their start and end apart: 9 -> 10, of which waited for: 7 -> 0; matrix products, arithmetic and copies ran while one was open for 8% -> 9% of each run, Pallas kernels for 0% -> 19%
where the time goes in v1:
time: 750 us; the launch traced here: 739 us
  Pallas kernels  293 us (39%)
  matrix products  146 us (19%)
  local copies, waits for them, and re-layouts  143 us (19%)
  blocking collectives  80.8 us (11%)
  other arithmetic  62 us (8%)
  starting transfers between devices  9.85 us (1%)
    pallas_call x1, Pallas kernels, scatter_grads(): pl.pallas_call(scatter_kernel, out_shape=[jax.ShapeDtypeStruct((144, 4608...  156 us
    pallas_call x1, Pallas kernels, gather_weights(): pl.pallas_call(gather_kernel, out_shape=shapes, in_specs=[hbm] * 4, out_s...  137 us
    unnamed x176, local copies, waits for them, and re-layouts  38.4 us
    dot_general x5, matrix products, outer(): lax.dot_general(left, right, (((0,), (0,)), ((), ())), preferred_element_...  33.9 us
    all_gather x1, blocking collectives, body_fast(): acted_all = lax.all_gather(acted_group, 'dp', axis=0, tiled=True)  33.3 us
    all_gather x1, blocking collectives, body_fast(): back_all = lax.all_gather(mod_back, 'dp', axis=0, tiled=True)  30.8 us
  transfers between devices with their start and end apart: 10, of which 0 were waited for; matrix products, arithmetic and copies ran while one was open for 9% of the time, Pallas kernels for 19%

profile of v1, /device:TPU:0, one launch (start us, length us, event | category | flops | bytes accessed | tf_op | source)
XLA Modules:
  0.0 738.6 jit_solution(12177501373628821107)
XLA Ops:
  2.4 6.2 all-gather
  19.2 33.3 %all_gather.10 = bf16[64,1152]{1,0:T(8,128)(2,1)} all-gather(bf16[8,1152]{1,0:T(8,128)(2,1)S(1)} %reshape.407), channel_id=1, replica_groups=mesh['dp'=8,'mod'=4] {'dp'}, dimensions={0}, use_global_device_ids=true | all-gather | bytes 165888 | tf_op jit(solution)/shard_map/all_gather | solution.py:838
  54.9 137.3 %gather_weights.1 = (bf16[4,2,144,4608]{3,2,1,0:T(8,128)(2,1)S(1)}, bf16[4,2,144,3072]{3,2,1,0:T(8,128)(2,1)S(1)}, bf16[4,2,144,3072]{3,2,1,0:T(8,128)(2,1)S(1)}, bf16[4,2,384,1152]{3,2,1,0:T(8,128)(2,1)S(1)}) custom-call(bf16[144,4608]{1,0:T(8,128)(2,1)S(1)} %pad_maximum_fusion.12.refs_0_, bf16[144,3072]{1,0:T(8,128)(2,1)S(1)} %copy-done, ...), custom_call_target="tpu_custom_call" | custom-call | tf_op jit(solution)/shard_map/gather_weights/pallas_call | solution.py:403
  192.3 4.0 copy-done.3
  207.5 7.9 %fusion.2 = f32[2,256,3456]{2,1,0:T(8,128)S(1)} fusion(bf16[2,256,1152]{2,1,0:T(8,128)(2,1)S(1)} %fusion.23, bf16[1152,4608]{1,0:T(8,128)(2,1)} %bitcast.106), kind=kOutput, calls=%fused_computation.17 | convolution fusion | flops 4076863488 | bytes 16220160 | tf_op jit(solution)/shard_map/bsd,de->bse/dot_general | solution.py:87
  223.4 5.0 copy.186
  236.0 5.0 copy.182
  245.4 4.5 broadcast_multiply_fusion
  272.7 7.8 %fusion.72 = f32[2,256,3072]{2,1,0:T(8,128)} fusion(bf16[2,256,1152]{2,1,0:T(8,128)(2,1)} %add_convert_fusion.1, bf16[1152,3072,1]{1,0,2:T(8,128)(2,1)S(1)} %bitcast.125), kind=kOutput, calls=%fused_computation.181 | convolution fusion | flops 3623878656 | bytes 14548992 | tf_op jit(solution)/shard_map/bsd,df->bsf/dot_general | solution.py:109
  280.5 7.6 %fusion.73 = f32[2,256,3072]{2,1,0:T(8,128)} fusion(bf16[2,256,1152]{2,1,0:T(8,128)(2,1)} %add_convert_fusion.1, bf16[1152,3072,1]{1,0,2:T(8,128)(2,1)S(1)} %bitcast.121), kind=kOutput, calls=%fused_computation.182 | convolution fusion | flops 3623878656 | bytes 14548992 | tf_op jit(solution)/shard_map/bsd,df->bsf/dot_general | solution.py:112
  289.3 13.8 %multiply_convert_fusion.1 = (bf16[2,256,3072]{2,1,0:T(8,128)(2,1)}, bf16[2,256,3072]{2,1,0:T(8,128)(2,1)}, bf16[2,256,3072]{2,1,0:T(8,128)(2,1)}) fusion(f32[2,256,3072]{2,1,0:T(8,128)} %fusion.72, f32[2,256,3072]{2,1,0:T(8,128)} %fusion.73, bf16[2,256,1152]{2,1,0:T(8,128)(2,1)} %fusion.30, bf16[3072,1152,1]{1,0,2:T(8,128)(2,1)} %bitcast.114), kind=kOutput, calls=%fused_computation.11 | convolution fusion | flops 3647471616 | bytes 30277632 | tf_op jit(solution)/shard_map/bsd,fd->bsf/dot_general | solution.py:121
  303.2 9.8 %fusion.74 = f32[2,256,1152]{2,1,0:T(8,128)} fusion(bf16[2,256,3072]{2,1,0:T(8,128)(2,1)} %get-tuple-element.37, bf16[1152,3072,1]{1,0,2:T(8,128)(2,1)} %bitcast.122), kind=kOutput, calls=%fused_computation.183 | convolution fusion | flops 3623878656 | bytes 12582912 | tf_op jit(solution)/shard_map/bsf,df->bsd/dot_general | solution.py:126
  313.0 12.0 %multiply_reduce_fusion.2 = (bf16[2,1152]{1,0:T(2,128)(2,1)}, f32[2,256]{1,0:T(2,128)S(1)}, bf16[2,1152]{1,0:T(2,128)(2,1)}, f32[2,256,1152]{2,1,0:T(8,128)}) fusion(f32[2,256,1152]{2,1,0:T(8,128)} %copy-done.34, f32[2,256]{1,0:T(2,128)S(1)} %add_rsqrt_fusion.2, f32[2,1152]{1,0:T(2,128)S(1)} %copy-done.59, f32[2,256,1152]{2,1,0:T(8,128)} %fusion.74, ...), kind=kOutput, calls=%fused_computation.76 | convolution fusion | flops 3628592128 | bytes 17324032 | tf_op jit(solution)/shard_map/bsf,df->bsd/dot_general | solution.py:129
  325.0 10.5 %fusion.31 = (bf16[2,1152]{1,0:T(2,128)(2,1)}, bf16[2,256,1152]{2,1,0:T(8,128)(2,1)}, bf16[2,1152]{1,0:T(2,128)(2,1)}, f32[2,256,1152]{2,1,0:T(8,128)S(1)}) fusion(bf16[2,256,1152]{2,1,0:T(8,128)(2,1)S(1)} %copy-done.39, f32[2,256,1152]{2,1,0:T(8,128)} %copy-done.34, f32[2,1152]{1,0:T(2,128)S(1)} %copy-done.57, f32[2,256,1152]{2,1,0:T(8,128)} %get-tuple-element.92, ...), kind=kOutput, calls=%fused_computation.59 | convolution fusion | flops 3632131584 | bytes 22051840 | tf_op jit(solution)/shard_map/bsf,fd->bsd/dot_general | solution.py:116
  343.6 6.4 convolution_convert_fusion.7
  350.0 4.8 multiply_reduce_fusion
  362.2 8.7 %copy.226 = bf16[2,256,3072]{1,0,2:T(2,128)(2,1)} copy(bf16[2,256,3072]{2,1,0:T(8,128)(2,1)} %get-tuple-element.38) | data formatting | bytes 6291456 | tf_op jit(solution)/shard_map/convert_element_type | solution.py:115
  390.6 5.0 copy.203
  406.8 4.4 multiply_reduce_fusion.4
  411.2 5.0 copy.213
  420.9 9.0 %multiply_convert_fusion.6 = (bf16[2,256,1152]{2,1,0:T(8,128)(2,1)}, bf16[2,256,1152]{2,1,0:T(8,128)(2,1)}) fusion(f32[2,256,1152]{2,1,0:T(8,128)} %copy.204, f32[2,256,1152]{2,1,0:T(8,128)} %copy.203, f32[2,256,1152]{2,1,0:T(8,128)} %copy.202, f32[2,256,3456]{2,1,0:T(8,128)} %copy-done.10, f32[2,256,1152]{2,1,0:T(8,128)} %copy.214, ...), kind=kLoop, calls=%fused_computation.81 | loop fusion | flops 5898240 | bytes 21233664 | tf_op jit(solution)/shard_map/convert.19
  430.6 8.7 %fusion.28 = (bf16[2,1152]{1,0:T(2,128)(2,1)S(1)}, f32[2,256]{1,0:T(2,128)S(1)}, bf16[2,1152]{1,0:T(2,128)(2,1)S(1)}, f32[2,256,1152]{2,1,0:T(8,128)}) fusion(bf16[2,256,1152]{2,1,0:T(8,128)(2,1)} %param.11, f32[2,256]{1,0:T(2,128)S(1)} %add_rsqrt_fusion.3, f32[2,1152]{1,0:T(2,128)S(1)} %get-tuple-element.81, bf16[1152,4608]{1,0:T(8,128)(2,1)S(1)} %bitcast.113, ...), kind=kOutput, calls=%fused_computation.56 | convolution fusion | flops 4092193792 | bytes 15063040 | tf_op jit(solution)/shard_map/bse,de->bsd/dot_general | solution.py:185
  440.8 4.0 all-to-all-start.1
  478.8 30.8 %all_gather.11 = bf16[64,1728]{1,0:T(8,128)(2,1)S(1)} all-gather(bf16[8,1728]{1,0:T(8,128)(2,1)S(1)} %all_to_all.26), channel_id=1, replica_groups=mesh['dp'=8,'mod'=4] {'dp'}, dimensions={0}, use_global_device_ids=true | all-gather | bytes 248832 | tf_op jit(solution)/shard_map/all_gather | solution.py:839
  514.6 10.5 %all-reduce = bf16[8,1152]{1,0:T(8,128)(2,1)S(1)} all-reduce(bf16[8,1152]{1,0:T(8,128)(2,1)S(1)} %convolution_convert_fusion.6), channel_id=2, replica_groups=mesh['dp'=8,'mod'=4] {'mod'}, use_global_device_ids=true, to_apply=%region_17.18.clone | all-reduce | flops 9216 | bytes 36864
  526.9 8.5 %convolution_convert_fusion.2 = bf16[1152,1536]{1,0:T(8,128)(2,1)} fusion(bf16[512,1536]{1,0:T(8,128)(2,1)} %collective-permute-done.4, bf16[512,1536]{1,0:T(8,128)(2,1)} %get-tuple-element.51, bf16[512,1152]{1,0:T(8,128)(2,1)} %collective-permute-done.3, bf16[512,1152]{1,0:T(8,128)(2,1)} %bitcast.42), kind=kOutput, calls=%fused_computation.7 | convolution fusion | flops 3636658176 | bytes 9043968 | tf_op jit(solution)/shard_map/dot_general | solution.py:816
  535.5 7.9 %convolution_convert_fusion.1 = bf16[1152,1536]{1,0:T(8,128)(2,1)} fusion(bf16[512,1536]{1,0:T(8,128)(2,1)} %collective-permute-done.5, bf16[512,1536]{1,0:T(8,128)(2,1)S(1)} %copy-done.38, bf16[512,1152]{1,0:T(8,128)(2,1)} %collective-permute-done.3, bf16[512,1152]{1,0:T(8,128)(2,1)} %bitcast.42), kind=kOutput, calls=%fused_computation.6 | convolution fusion | flops 3636658176 | bytes 9043968 | tf_op jit(solution)/shard_map/dot_general | solution.py:816
  543.4 8.4 %convolution_convert_fusion = bf16[1536,1152]{1,0:T(8,128)(2,1)} fusion(bf16[512,1536]{0,1:T(8,128)(2,1)} %collective-permute-done.6, bf16[512,1536]{0,1:T(8,128)(2,1)S(1)} %get-tuple-element.47, bf16[512,1152]{1,0:T(8,128)(2,1)S(1)} %collective-permute-done.7, bf16[512,1152]{1,0:T(8,128)(2,1)S(1)} %bitcast.168), kind=kOutput, calls=%fused_computation.5 | convolution fusion | flops 3636658176 | bytes 9043968 | tf_op jit(solution)/shard_map/dot_general | solution.py:816
  551.8 4.6 convolution_convert_fusion.4
  556.5 4.6 convolution_convert_fusion.3
  563.8 8.6 %copy.225 = bf16[1152,2304]{1,0:T(8,128)(2,1)} copy(bf16[1152,2304]{0,1:T(8,128)(2,1)} %pad_maximum_fusion) | data formatting | bytes 10616832 | tf_op jit(solution)/shard_map/concatenate | solution.py:823
  572.4 156.1 %scatter_grads.1 = (f32[144,4608]{1,0:T(8,128)}, f32[144,3072]{1,0:T(8,128)}, f32[144,3072]{1,0:T(8,128)}, f32[384,1152]{1,0:T(8,128)}) custom-call(bf16[4,2,144,2304]{3,2,1,0:T(8,128)(2,1)} %bitcast.128, bf16[4,2,144,1536]{3,2,1,0:T(8,128)(2,1)} %bitcast.162, bf16[4,2,144,1536]{3,2,1,0:T(8,128)(2,1)} %bitcast.163, bf16[4,2,192,1152]{3,2,1,0:T(8,128)(2,1)} %bitcast.164), custom_call_target="tpu_custom_call" | custom-call | tf_op jit(solution)/shard_map/scatter_grads/pallas_call | solution.py:607
  (293 shorter events, 175.4 us)
Async XLA Ops:
  0.6 16.0 %copy-start.12 = (bf16[2,256,1152]{2,1,0:T(8,128)(2,1)S(1)}, bf16[2,256,1152]{2,1,0:T(8,128)(2,1)}, u32[]{:S(2)}) copy-start(bf16[2,256,1152]{2,1,0:T(8,128)(2,1)} %param.11) | copy-start | bytes 3538948
  12.6 39.8 %copy-start.67 = (u32[32]{0:T(128)S(1)}, u32[32]{0:T(128)}, u32[]{:S(2)}) copy-start(u32[32]{0:T(128)} %constant.109) | copy-start | bytes 388
  12.6 41.1 %copy-start = (bf16[144,3072]{1,0:T(8,128)(2,1)S(1)}, bf16[144,3072]{1,0:T(8,128)(2,1)}, u32[]{:S(2)}) copy-start(bf16[144,3072]{1,0:T(8,128)(2,1)} %refs_1_.1) | copy-start | bytes 2654212
  12.7 41.1 %copy-start.1 = (bf16[144,3072]{1,0:T(8,128)(2,1)S(1)}, bf16[144,3072]{1,0:T(8,128)(2,1)}, u32[]{:S(2)}) copy-start(bf16[144,3072]{1,0:T(8,128)(2,1)} %refs_2_.1) | copy-start | bytes 2654212
  13.3 191.6 %all-to-all-start = ((bf16[4,2,1728]{2,1,0:T(2,128)(2,1)}), bf16[4,2,1728]{2,1,0:T(2,128)(2,1)S(1)}, u32[]{:S(2)}, u32[]{:S(2)}) async-start(bf16[4,2,1728]{2,1,0:T(2,128)(2,1)} %all_to_all.22), calls=%async_computation | async-start | bytes 57344 | tf_op jit(solution)/shard_map/all_to_all | solution.py:782
  264.2 8.5 %slice-start.10 = ((s8[7077888]{0:T(1024)(128)(4,1)}), s8[4194304]{0:T(1024)(128)(4,1)S(1)}, s32[]{:S(2)}) async-start(s8[7077888]{0:T(1024)(128)(4,1)} %bitcast.123), calls=%async_computation.12 | async-start | bytes 8388608
  271.3 9.2 %slice-start.8 = ((s8[7077888]{0:T(1024)(128)(4,1)}), s8[4194304]{0:T(1024)(128)(4,1)S(1)}, s32[]{:S(2)}) async-start(s8[7077888]{0:T(1024)(128)(4,1)} %bitcast.119), calls=%async_computation.10 | async-start | bytes 8388608
  303.2 21.8 %slice-start.6 = ((s8[7077888]{0:T(1024)(128)(4,1)}), s8[4194304]{0:T(1024)(128)(4,1)S(1)}, s32[]{:S(2)}) async-start(s8[7077888]{0:T(1024)(128)(4,1)} %bitcast.115), calls=%async_computation.8 | async-start | bytes 8388608
  313.0 12.0 %slice-start.7 = ((s8[7077888]{0:T(1024)(128)(4,1)}), s8[2883584]{0:T(1024)(128)(4,1)S(1)}, s32[]{:S(2)}) async-start(s8[7077888]{0:T(1024)(128)(4,1)} %bitcast.115), calls=%async_computation.9 | async-start | bytes 5767168
  343.6 11.2 %slice-start.12 = ((s8[8388608]{0:T(1024)(128)(4,1)}), s8[4194304]{0:T(1024)(128)(4,1)S(1)}, s32[]{:S(2)}) async-start(s8[8388608]{0:T(1024)(128)(4,1)} %bitcast.126), calls=%async_computation.14 | async-start | bytes 8388608
  362.2 8.7 %copy-start.16 = (bf16[2,16,72,256]{3,2,1,0:T(8,128)(2,1)S(1)}, bf16[2,16,72,256]{3,2,1,0:T(8,128)(2,1)}, u32[]{:S(2)}) copy-start(bf16[2,16,72,256]{3,2,1,0:T(8,128)(2,1)} %convolution_convert_fusion.7) | copy-start | bytes 3538948
  416.2 13.6 %slice-start.3 = ((s8[10616832]{0:T(1024)(128)(4,1)}), s8[2228224]{0:T(1024)(128)(4,1)S(1)}, s32[]{:S(2)}) async-start(s8[10616832]{0:T(1024)(128)(4,1)} %bitcast.111), calls=%async_computation.5 | async-start | bytes 4456448
  420.9 9.0 %slice-start.4 = ((s8[10616832]{0:T(1024)(128)(4,1)}), s8[4194304]{0:T(1024)(128)(4,1)S(1)}, s32[]{:S(2)}) async-start(s8[10616832]{0:T(1024)(128)(4,1)} %bitcast.111), calls=%async_computation.6 | async-start | bytes 8388608
  420.9 9.7 %slice-start.5 = ((s8[10616832]{0:T(1024)(128)(4,1)}), s8[4194304]{0:T(1024)(128)(4,1)S(1)}, s32[]{:S(2)}) async-start(s8[10616832]{0:T(1024)(128)(4,1)} %bitcast.111), calls=%async_computation.7 | async-start | bytes 8388608
  430.6 9.4 %copy-start.66 = (bf16[2,1152]{1,0:T(2,128)(2,1)S(1)}, bf16[2,1152]{1,0:T(2,128)(2,1)}, u32[]{:S(2)}) copy-start(bf16[2,1152]{1,0:T(2,128)(2,1)} %get-tuple-element.63) | copy-start | bytes 13828
  430.6 9.4 %copy-start.64 = (bf16[2,1152]{1,0:T(2,128)(2,1)S(1)}, bf16[2,1152]{1,0:T(2,128)(2,1)}, u32[]{:S(2)}) copy-start(bf16[2,1152]{1,0:T(2,128)(2,1)} %get-tuple-element.30) | copy-start | bytes 13828
  430.6 9.4 %copy-start.63 = (bf16[2,1152]{1,0:T(2,128)(2,1)S(1)}, bf16[2,1152]{1,0:T(2,128)(2,1)}, u32[]{:S(2)}) copy-start(bf16[2,1152]{1,0:T(2,128)(2,1)} %get-tuple-element.26) | copy-start | bytes 13828
  430.6 9.4 %copy-start.65 = (bf16[2,1152]{1,0:T(2,128)(2,1)S(1)}, bf16[2,1152]{1,0:T(2,128)(2,1)}, u32[]{:S(2)}) copy-start(bf16[2,1152]{1,0:T(2,128)(2,1)} %get-tuple-element.61) | copy-start | bytes 13828
  440.8 37.2 %all-to-all-start.1 = ((bf16[2,4,1728]{2,0,1:T(2,128)(2,1)}), bf16[2,4,1728]{2,0,1:T(2,128)(2,1)}, u32[]{:S(2)}, u32[]{:S(2)}) async-start(bf16[2,4,1728]{2,0,1:T(2,128)(2,1)} %copy.217), calls=%async_computation.1 | async-start | bytes 57344 | tf_op jit(solution)/shard_map/all_to_all | solution.py:837
  456.0 95.8 %collective-permute-start.1 = (bf16[512,2304]{0,1:T(8,128)(2,1)}, bf16[512,2304]{0,1:T(8,128)(2,1)}, u32[]{:S(2)}, u32[]{:S(2)}) collective-permute-start(bf16[512,2304]{0,1:T(8,128)(2,1)} %get-tuple-element.46), channel_id=1, source_target_pairs={{0,1},{1,0},{2,3},{3,2},{4,5},{5,4},{6,7},{7,6},{8,9},{9,8},{10,11... | collective-permute-start | bytes 7077896 | tf_op jit(solution)/shard_map/ppermute | solution.py:746
  458.7 67.9 %collective-permute-start.4 = (bf16[512,1536]{1,0:T(8,128)(2,1)}, bf16[512,1536]{1,0:T(8,128)(2,1)}, u32[]{:S(2)}, u32[]{:S(2)}) collective-permute-start(bf16[512,1536]{1,0:T(8,128)(2,1)} %get-tuple-element.52), channel_id=1, source_target_pairs={{0,1},{1,0},{2,3},{3,2},{4,5},{5,4},{6,7},{7,6},{8,9},{9,8},{10,11... | collective-permute-start | bytes 4718600 | tf_op jit(solution)/shard_map/ppermute | solution.py:746
  459.1 67.3 %collective-permute-start.3 = (bf16[512,1152]{1,0:T(8,128)(2,1)}, bf16[512,1152]{1,0:T(8,128)(2,1)}, u32[]{:S(2)}, u32[]{:S(2)}) collective-permute-start(bf16[512,1152]{1,0:T(8,128)(2,1)} %bitcast.42), channel_id=1, source_target_pairs={{0,1},{1,0},{2,3},{3,2},{4,5},{5,4},{6,7},{7,6},{8,9},{9,8},{10,11... | collective-permute-start | bytes 3538952 | tf_op jit(solution)/shard_map/ppermute | solution.py:746
  467.1 76.3 %collective-permute-start.6 = (bf16[512,1536]{0,1:T(8,128)(2,1)}, bf16[512,1536]{0,1:T(8,128)(2,1)}, u32[]{:S(2)}, u32[]{:S(2)}) collective-permute-start(bf16[512,1536]{0,1:T(8,128)(2,1)} %get-tuple-element.48), channel_id=1, source_target_pairs={{0,1},{1,0},{2,3},{3,2},{4,5},{5,4},{6,7},{7,6},{8,9},{9,8},{10,11... | collective-permute-start | bytes 4718600 | tf_op jit(solution)/shard_map/ppermute | solution.py:746
  477.6 57.8 %collective-permute-start.5 = (bf16[512,1536]{1,0:T(8,128)(2,1)}, bf16[512,1536]{1,0:T(8,128)(2,1)}, u32[]{:S(2)}, u32[]{:S(2)}) collective-permute-start(bf16[512,1536]{1,0:T(8,128)(2,1)} %get-tuple-element.50), channel_id=1, source_target_pairs={{0,1},{1,0},{2,3},{3,2},{4,5},{5,4},{6,7},{7,6},{8,9},{9,8},{10,11... | collective-permute-start | bytes 4718600 | tf_op jit(solution)/shard_map/ppermute | solution.py:746
  511.8 13.9 %copy-start.54 = (f32[2,576]{1,0:T(2,128)S(1)}, f32[2,576]{1,0:T(2,128)}, u32[]{:S(2)}) copy-start(f32[2,576]{1,0:T(2,128)} %copy-done.53) | copy-start | bytes 13828
  511.8 13.9 %copy-start.56 = (f32[2,576]{1,0:T(2,128)S(1)}, f32[2,576]{1,0:T(2,128)}, u32[]{:S(2)}) copy-start(f32[2,576]{1,0:T(2,128)} %copy-done.55) | copy-start | bytes 13828
  511.8 13.9 %copy-start.61 = (bf16[2,1152]{1,0:T(2,128)(2,1)S(1)}, bf16[2,1152]{1,0:T(2,128)(2,1)}, u32[]{:S(2)}) copy-start(bf16[2,1152]{1,0:T(2,128)(2,1)} %param.12) | copy-start | bytes 13828
  526.4 30.0 %collective-permute-start.2 = (bf16[512,1152]{0,1:T(8,128)(2,1)}, bf16[512,1152]{0,1:T(8,128)(2,1)S(1)}, u32[]{:S(2)}, u32[]{:S(2)}) collective-permute-start(bf16[512,1152]{0,1:T(8,128)(2,1)} %bitcast.169), channel_id=1, source_target_pairs={{0,1},{1,0},{2,3},{3,2},{4,5},{5,4},{6,7},{7,6},{8,9},{9,8},{10,11... | collective-permute-start | bytes 3538952 | tf_op jit(solution)/shard_map/ppermute | solution.py:746
  526.5 16.9 %collective-permute-start.7 = (bf16[512,1152]{1,0:T(8,128)(2,1)}, bf16[512,1152]{1,0:T(8,128)(2,1)S(1)}, u32[]{:S(2)}, u32[]{:S(2)}) collective-permute-start(bf16[512,1152]{1,0:T(8,128)(2,1)} %bitcast.167), channel_id=1, source_target_pairs={{0,1},{1,0},{2,3},{3,2},{4,5},{5,4},{6,7},{7,6},{8,9},{9,8},{10,11... | collective-permute-start | bytes 3538952 | tf_op jit(solution)/shard_map/ppermute | solution.py:746
  526.9 8.5 %copy-start.42 = (bf16[512,1152]{0,1:T(8,128)(2,1)S(1)}, bf16[512,1152]{0,1:T(8,128)(2,1)}, u32[]{:S(2)}) copy-start(bf16[512,1152]{0,1:T(8,128)(2,1)} %copy.219) | copy-start | bytes 3538948
  526.9 8.6 %copy-start.38 = (bf16[512,1536]{1,0:T(8,128)(2,1)S(1)}, bf16[512,1536]{1,0:T(8,128)(2,1)}, u32[]{:S(2)}) copy-start(bf16[512,1536]{1,0:T(8,128)(2,1)} %get-tuple-element.49) | copy-start | bytes 4718596
  535.4 16.4 %collective-permute-start = (bf16[512,1152]{0,1:T(8,128)(2,1)S(1)}, bf16[512,1152]{0,1:T(8,128)(2,1)S(1)}, u32[]{:S(2)}, u32[]{:S(2)}) collective-permute-start(bf16[512,1152]{0,1:T(8,128)(2,1)S(1)} %copy-done.42), channel_id=1, source_target_pairs={{0,1},{1,0},{2,3},{3,2},{4,5},{5,4},{6,7},{7,6},{8,9},{9,8},{10,11... | collective-permute-start | bytes 3538952 | tf_op jit(solution)/shard_map/ppermute | solution.py:746
  (60 other events, 229.4 us)

commit v2 on v1

--- a/solution.py
+++ b/solution.py
@@ -1,4 +1,6 @@
 import math
+from types import SimpleNamespace
+from typing import NamedTuple
 
 import jax
 import jax.numpy as jnp
@@ -271,8 +273,9 @@
 
 
 class Gather:
-    def __init__(self, refs, sems, spot):
+    def __init__(self, refs, sems, spot, stages):
         self.z, self.x, self.y, self.c = spot
+        self.stages = stages
         self.pieces = gather_pieces(refs, self.c, lambda rows, j: rows // 3)
         self.send_sems, self.recv_sems, self.own_sems = sems
         self.refs = refs
@@ -289,13 +292,18 @@
 
     def own_copies(self):
         for k in range(4):
+            pltpu.make_async_copy(self.refs[k], self.stages[k], self.own_sems.at[k]).start()
+
+    def own_stores(self):
+        for k in range(4):
+            drain(self.stages[k], self.own_sems.at[k])
             pltpu.make_async_copy(
-                self.refs[k], self.refs[4 + k].at[self.z, self.x], self.own_sems.at[k]
+                self.stages[k], self.refs[4 + k].at[self.z, self.x], self.own_sems.at[k]
             ).start()
 
     def own_done(self):
         for k in range(4):
-            drain(self.refs[k], self.own_sems.at[k])
+            drain(self.stages[k], self.own_sems.at[k])
 
     def start_z(self, t):
         p = self.pieces[t]
@@ -368,14 +376,431 @@
 N_PIECES = 17
 
 
-def gather_kernel(*refs):
-    arrays, sems = refs[:8], refs[8:]
+TOK = 512
+TILE = 64
+ATTN_STEPS = 8
+
+
+def mm(left, right):
+    return lax.dot_general(left, right, (((1,), (0,)), ((), ())), preferred_element_type=F32)
+
+
+def mm_nt(left, right):
+    return lax.dot_general(left, right, (((1,), (1,)), ((), ())), preferred_element_type=F32)
+
+
+def mm_tn(left, right):
+    return lax.dot_general(left, right, (((0,), (0,)), ((), ())), preferred_element_type=F32)
+
+
+def split(value):
+    high = value.astype(BF16)
+    return high, (value - high.astype(F32)).astype(BF16)
+
+
+def mm_split(value, right):
+    high, low = split(value)
+    return mm(high, right) + mm(low, right)
+
+
+def partner(value, first):
+    width = value.shape[1]
+    return jnp.where(first, pltpu.roll(value, width - 18, 1), pltpu.roll(value, 18, 1))
+
+
+def first_lanes(rows):
+    return lax.broadcasted_iota(jnp.int32, (rows, D), 1) % 36 < 18
+
+
+def rows_of(block, count):
+    return pl.ds(pl.multiple_of(block * count, count), count)
+
+
+def head_window(head):
+    base = jnp.minimum(head * HD // 128 * 128, D - 256)
+    offset = head * HD - base
+    lane = lax.broadcasted_iota(jnp.int32, (SEQ, 256), 1)
+    mask = (lane >= offset) & (lane < offset + HD)
+    return pl.ds(pl.multiple_of(base, 128), 256), mask
+
+
+def flat(ref_value):
+    return ref_value.reshape(-1, ref_value.shape[-1])
+
+
+class Saves:
+    def __init__(self, sems):
+        self.sems, self.count, self.open = sems, 0, []
+
+    def local(self, source, target):
+        copy = pltpu.make_async_copy(source, target, self.sems.at[self.count])
+        self.count += 1
+        copy.start()
+        self.open.append(copy)
+        return copy
+
+    def done(self, copy):
+        copy.wait()
+        self.open = [other for other in self.open if other is not copy]
+
+    def finish(self):
+        for copy in self.open:
+            copy.wait()
+
+
+class Forward:
+    def __init__(self, s, spot, gather):
+        self.s, self.gather = s, gather
+        self.z, self.x, self.y, self.c = spot
+        self.saves = Saves(s.save_sems)
+        self.pending = {}
+        self.remote = []
+        self.slots = {}
+
+
+    def to_sibling(self, source, target):
+        k = len(self.remote)
+        peer = device(self.z, self.x, self.y, 1 - self.c)
+        copy = pltpu.make_async_remote_copy(
+            src_ref=source,
+            dst_ref=target,
+            send_sem=self.s.pair_send.at[k],
+            recv_sem=self.s.pair_recv.at[k],
+            device_id=peer,
+            device_id_type=MESH,
+        )
+        copy.start()
+        self.remote.append(copy)
+
+
+    def load(self, key, part, source, target):
+        if (key, part) not in self.pending:
+            copy = pltpu.make_async_copy(source, target, self.s.load_sems.at[len(self.pending)])
+            copy.start()
+            self.pending[key, part] = copy
+
+    def window(self, ref, column):
+        return ref.at[:, :, :, pl.ds(column, WIDTH)]
+
+    def load_qv(self, j):
+        packed = self.gather.refs[4]
+        self.load(j, 0, self.window(packed, j * WIDTH), self.s.w.at[j % 2, 0])
+        self.load(j, 1, self.window(packed, LANE_HALF + j * WIDTH), self.s.w.at[j % 2, 1])
+
+    def load_ko(self, j):
+        packed = self.gather.refs[4]
+        self.load(j, 0, self.window(packed, j * WIDTH), self.s.w.at[j % 2, 0])
+        target = self.window(self.s.w_out, (j - 3) * WIDTH)
+        self.load(j, 1, self.window(packed, LANE_HALF + j * WIDTH), target)
+
+    def load_ff(self, j):
+        at = (j // 2 + 4 * (j % 2)) * WIDTH
+        self.load(6 + j, 0, self.window(self.gather.refs[5], at), self.s.w.at[j % 2, 0])
+        self.load(6 + j, 1, self.window(self.gather.refs[6], at), self.s.w.at[j % 2, 1])
+
+    def load_down(self, j):
+        self.load(14 + j, 0, self.window(self.gather.refs[7], j * WIDTH), self.s.w_down.at[j % 2])
+
+    def loaded(self, load, j, key):
+        load(j)
+        for part in range(2):
+            if (key, part) in self.pending:
+                self.pending[key, part].wait()
+
+
+    def enter(self):
+        s = self.s
+
+        @pl.loop(0, TOK // TILE)
+        def _(i):
+            rows = rows_of(i, TILE)
+            image = i // (SEQ // TILE)
+            mod = s.mod
+            normed, _ = norm_rows(s.tokens[rows, :].astype(F32))
+            entry = normed * (1.0 + mod[image, 1:2, :]) + mod[image, 0:1, :]
+            s.entry_a[rows, :] = entry.astype(BF16)
+            branch = mod[image, 5:6, :] * s.cot[rows, :].astype(F32)
+            s.d_branch[rows, :] = branch.astype(BF16)
+
+        self.saves.local(s.d_branch, s.o_branch.at[pl.ds(0, TOK)])
+        self.to_sibling(s.d_branch, s.o_branch.at[pl.ds(TOK, TOK)])
+        self.turn(s.entry_a, s.t_a)
+        self.share(s.t_a, s.o_lhs.at[0])
+
+    def turn(self, source, target):
+        @pl.loop(0, source.shape[1] // 128)
+        def _(i):
+            columns = rows_of(i, 128)
+            target[columns, :] = source[:, columns].T
+
+    def share(self, source, target):
+        self.saves.local(source, target.at[:, pl.ds(0, TOK)])
+        self.to_sibling(source, target.at[:, pl.ds(TOK, TOK)])
+
+    def qv(self, j):
+        s = self.s
+        self.loaded(self.load_qv, j, j)
+        columns = pl.ds(j * WIDTH, WIDTH)
+        s.proj[:, columns] = mm(s.entry_a[...], flat(s.w[j % 2, 0]))
+        s.v[:, columns] = mm(s.entry_a[...], flat(s.w[j % 2, 1])).astype(BF16)
+        if j == 2:
+            self.saves.local(s.v, s.o_qkv.at[2])
+
+    def ko(self, j):
+        s = self.s
+        self.loaded(self.load_ko, j, j)
+        columns = pl.ds((j - 3) * WIDTH, WIDTH)
+        s.proj[:, columns] = mm(s.entry_a[...], flat(s.w[j % 2, 0]))
+
+    def head_norm(self, which):
+        s = self.s
+        target, normed = (s.q, s.q_normed) if which == 0 else (s.k, s.k_normed)
+        scale = s.scale_q if which == 0 else s.scale_k
+
+        @pl.loop(0, TOK // TILE)
+        def _(i):
+            rows = rows_of(i, TILE)
+            spots = rows_of(i % (SEQ // TILE), TILE)
+            field = s.proj[rows, :]
+            inverse = lax.rsqrt(mm_split(field * field, s.spread[...]) * (1.0 / HD) + EPSILON)
+            scale[rows, :] = inverse
+            field = field * mm_split(inverse, s.widen[...])
+            normed[rows, :] = field.astype(BF16)
+            turned = field * s.cos[spots, :] + partner(field, first_lanes(TILE)) * s.sin[spots, :]
+            target[rows, :] = turned.astype(BF16)
+
+        self.saves.local(target, s.o_qkv.at[which])
+        self.saves.local(normed, s.o_normed.at[which])
+        self.saves.local(scale, s.o_scale.at[which])
+
+    def attend(self, k):
+        s = self.s
+        heads = H // ATTN_STEPS
+        if k >= 2:
+            self.saves.done(self.slots[k - 2])
+
+        @pl.loop(0, heads)
+        def _(i):
+            window, mask = head_window(k * heads + i)
+            for image in range(2):
+                rows = pl.ds(image * SEQ, SEQ)
+                query = jnp.where(mask, s.q[rows, window].astype(F32), 0.0).astype(BF16)
+                scores = mm_nt(query, s.k[rows, window]) * (1.0 / math.sqrt(HD))
+                powers = jnp.exp(scores - jnp.max(scores, axis=1, keepdims=True))
+                total = jnp.sum(powers, axis=1, keepdims=True)
+                soft = (powers * (1.0 / total)).astype(BF16)
+                s.soft[k % 2, i, image] = soft
+                mixed = mm(soft, s.v[rows, window])
+                old = s.combined[rows, window].astype(F32)
+                s.combined[rows, window] = jnp.where(mask, mixed, old).astype(BF16)
+
+        self.slots[k] = self.saves.local(s.soft.at[k % 2], s.o_soft.at[pl.ds(k * heads, heads)])
+
+    def leave(self):
+        s = self.s
+        self.saves.done(self.slots[ATTN_STEPS - 2])
+        self.saves.done(self.slots[ATTN_STEPS - 1])
+        self.turn(s.combined, s.t_c)
+        self.share(s.t_c, s.o_lhs.at[1])
+        for j in range(3):
+            columns = pl.ds(j * WIDTH, WIDTH)
+            s.proj[:, columns] = mm(s.combined[...], flat(s.w_out[:, :, :, columns]))
+
+        @pl.loop(0, TOK // TILE)
+        def _(i):
+            rows = rows_of(i, TILE)
+            image = i // (SEQ // TILE)
+            mod = s.mod
+            attended = s.proj[rows, :]
+            s.attended[rows, :] = attended.astype(BF16)
+            residual = s.tokens[rows, :].astype(F32) + mod[image, 2:3, :] * attended
+            s.residual[rows, :] = residual
+            normed, _ = norm_rows(residual)
+            entry = normed * (1.0 + mod[image, 4:5, :]) + mod[image, 3:4, :]
+            s.entry_b[rows, :] = entry.astype(BF16)
+
+        self.saves.local(s.attended, s.o_attended)
+        self.saves.local(s.residual, s.o_residual)
+        self.turn(s.entry_b, s.t_b)
+        self.share(s.t_b, s.o_lhs.at[2])
+
+    def ff(self, j):
+        s = self.s
+        self.loaded(self.load_ff, j, 6 + j)
+        shard = j // 2 + 4 * (j % 2)
+        at = shard * WIDTH
+        columns = pl.ds(at, WIDTH)
+        s.wide[0] = mm(s.entry_b[...], flat(s.w[j % 2, 0]))
+        s.wide[1] = mm(s.entry_b[...], flat(s.w[j % 2, 1]))
+        if (6, j - 2) in self.slots:
+            for copy in self.slots[(6, j - 2)]:
+                self.saves.done(copy)
+        slot = j % 2
+
+        @pl.loop(0, TOK // TILE)
+        def _(i):
+            rows = rows_of(i, TILE)
+            gate = s.wide[0, rows, :]
+            up = s.wide[1, rows, :]
+            sigma = 1.0 / (1.0 + jnp.exp(-gate))
+            active = gate * sigma
+            s.active[slot, 0, rows, :] = active.astype(BF16)
+            slope = up * sigma * (1.0 + gate * (1.0 - sigma))
+            s.active[slot, 1, rows, :] = slope.astype(BF16)
+            s.hidden[rows, columns] = (active * up).astype(BF16)
+
+        self.slots[(6, j)] = [
+            self.saves.local(s.active.at[slot], s.o_active.at[shard]),
+        ]
+        for i in range(3):
+            s.t_h[shard, 128 * i : 128 * i + 128, :] = s.hidden[:, at + 128 * i : at + 128 * i + 128].T
+        mine = pl.ds(pl.multiple_of(self.c * 192, 16), 192)
+        theirs = pl.ds(pl.multiple_of((1 - self.c) * 192, 16), 192)
+        self.saves.local(s.t_h.at[shard, mine], s.o_hidden.at[shard, :, pl.ds(0, TOK)])
+        self.to_sibling(s.t_h.at[shard, theirs], s.o_hidden.at[shard, :, pl.ds(TOK, TOK)])
+
+    def down(self, j):
+        s = self.s
+        self.loaded(self.load_down, j, 14 + j)
+        columns = pl.ds(j * WIDTH, WIDTH)
+        s.wide[0] = mm(s.hidden[...], flat(s.w_down[j % 2]))
+        for image in range(2):
+            gate = s.mod[image, 5:6, columns]
+            total = jnp.zeros((1, WIDTH), F32)
+            for i in range(SEQ // TILE):
+                rows = pl.ds(image * SEQ + i * TILE, TILE)
+                branch = s.wide[0, rows, :]
+                result = s.residual[rows, columns] + gate * branch
+                s.result[rows, columns] = result.astype(BF16)
+                total = total + jnp.sum(
+                    s.cot[rows, columns].astype(F32) * branch, axis=0, keepdims=True
+                )
+            s.o_gate_b[image, 0:1, columns] = total
+        if j == 2:
+            self.saves.local(s.result, s.o_result)
+
+    def plan(self):
+        steps = [(None, self.enter, None, 0, 4)]
+        steps += [(self.load_qv, self.qv, j, j + 1, 2.5) for j in range(3)]
+        steps += [(None, self.head_norm, 0, 3, 8)]
+        steps += [(self.load_ko, self.ko, j, j + 1, 1.5) for j in range(3, 6)]
+        steps += [(None, self.head_norm, 1, 6, 8)]
+        steps += [(None, self.attend, k, 6, 3) for k in range(ATTN_STEPS)]
+        steps += [(None, self.leave, None, 6, 8)]
+        steps += [(self.load_ff, self.ff, j, 8 + 2 * (j // 2), 4.5) for j in range(8)]
+        steps += [(self.load_down, self.down, j, 15 + j, 4) for j in range(3)]
+        return steps
+
+    def finish(self):
+        self.saves.finish()
+        for copy in self.remote:
+            copy.wait_send()
+            copy.wait_recv()
+
+
+class ForwardInputs(NamedTuple):
+    packed: object
+    gate: object
+    up: object
+    down: object
+    tokens: object
+    cot: object
+    mod: object
+    cos: object
+    sin: object
+    spread: object
+    widen: object
+
+
+FORWARD_OUTPUTS = dict(
+    packed_all=((4, 2, 144, 4608), BF16),
+    gate_all=((4, 2, 144, 3072), BF16),
+    up_all=((4, 2, 144, 3072), BF16),
+    down_all=((4, 2, 384, 1152), BF16),
+    o_branch=((2 * TOK, D), BF16),
+    o_lhs=((3, D, 2 * TOK), BF16),
+    o_hidden=((8, 192, 2 * TOK), BF16),
+    o_qkv=((3, TOK, D), BF16),
+    o_normed=((2, TOK, D), BF16),
+    o_scale=((2, TOK, 128), F32),
+    o_soft=((H, 2, SEQ, SEQ), BF16),
+    o_attended=((TOK, D), BF16),
+    o_residual=((TOK, D), F32),
+    o_active=((8, 2, TOK, WIDTH), BF16),
+    o_result=((TOK, D), BF16),
+    o_gate_b=((2, 8, D), F32),
+)
+
+
+def forward_scratch():
+    def vmem(*shape, kind=BF16):
+        return pltpu.VMEM(shape, kind)
+
+    return dict(
+        entry_a=vmem(TOK, D),
+        d_branch=vmem(TOK, D),
+        t_a=vmem(D, TOK),
+        proj=vmem(TOK, D, kind=F32),
+        q=vmem(TOK, D),
+        k=vmem(TOK, D),
+        v=vmem(TOK, D),
+        q_normed=vmem(TOK, D),
+        k_normed=vmem(TOK, D),
+        scale_q=vmem(TOK, 128, kind=F32),
+        scale_k=vmem(TOK, 128, kind=F32),
+        soft=vmem(2, H // ATTN_STEPS, 2, SEQ, SEQ),
+        combined=vmem(TOK, D),
+        t_c=vmem(D, TOK),
+        attended=vmem(TOK, D),
+        residual=vmem(TOK, D, kind=F32),
+        entry_b=vmem(TOK, D),
+        t_b=vmem(D, TOK),
+        wide=vmem(2, TOK, WIDTH, kind=F32),
+        active=vmem(2, 2, TOK, WIDTH),
+        hidden=vmem(TOK, 8 * WIDTH),
+        t_h=vmem(8, WIDTH, TOK),
+        result=vmem(TOK, D),
+        w=vmem(2, 2, 4, 2, 144, WIDTH),
+        w_out=vmem(4, 2, 144, D),
+        w_down=vmem(2, 4, 2, 384, WIDTH),
+        gather_send=pltpu.SemaphoreType.DMA((4, N_PIECES)),
+        gather_recv=pltpu.SemaphoreType.DMA((4, N_PIECES)),
+        own_packed=vmem(144, 4 * D),
+        own_gate=vmem(144, 8 * WIDTH),
+        own_up=vmem(144, 8 * WIDTH),
+        own_down=vmem(384, D),
+        own_sems=pltpu.SemaphoreType.DMA((4,)),
+        save_sems=pltpu.SemaphoreType.DMA((48,)),
+        load_sems=pltpu.SemaphoreType.DMA((48,)),
+        pair_send=pltpu.SemaphoreType.DMA((16,)),
+        pair_recv=pltpu.SemaphoreType.DMA((16,)),
+    )
+
+
+def run_step(steps, arrived):
+    _, act, j, _, cost = steps.pop(0)
+    if steps and steps[0][0] is not None and steps[0][3] <= arrived:
+        steps[0][0](steps[0][2])
+    act() if j is None else act(j)
+    return cost
+
+
+def forward_kernel(*refs):
+    names = ForwardInputs._fields + tuple(FORWARD_OUTPUTS) + tuple(forward_scratch())
+    s = SimpleNamespace(**dict(zip(names, refs, strict=True)))
     spot = place()
     greet(neighbours(*spot))
-    gather = Gather(arrays, sems, spot)
+    arrays = [s.packed, s.gate, s.up, s.down, s.packed_all, s.gate_all, s.up_all, s.down_all]
+    stages = [s.own_packed, s.own_gate, s.own_up, s.own_down]
+    gather = Gather(arrays, (s.gather_send, s.gather_recv, s.own_sems), spot, stages)
+    work = Forward(s, spot, gather)
+    steps = work.plan()
     gather.own_copies()
     ahead = 2
+    arrived = 0
     for t in range(N_PIECES + 4 + ahead):
+        if t == 1:
+            gather.own_stores()
         if t < N_PIECES:
             if t >= ahead:
                 gather.sent_z(t - ahead)
@@ -387,46 +812,62 @@
         if 0 <= t - ahead - 2 < N_PIECES:
             gather.start_c(t - ahead - 2)
         if 0 <= t - ahead - 3 < N_PIECES:
+            if arrived == 0:
+                gather.own_done()
             gather.arrived(t - ahead - 3)
+            arrived += 1
+        spent = 0.0
+        while steps and steps[0][3] <= arrived and spent < 6.0:
+            spent += run_step(steps, arrived)
+    while steps:
+        run_step(steps, arrived)
     for t in range(N_PIECES - ahead, N_PIECES):
         gather.sent_z(t)
     for t in range(N_PIECES):
         gather.sent_rest(t)
-    gather.own_done()
-
-
-def gather_weights(packed, gate, up, down):
+    work.finish()
+
+
+def forward_pass(packed, gate, up, down, tokens, cotangent, mod, tables):
     hbm = pl.BlockSpec(memory_space=pl.ANY)
-    shapes = [
-        jax.ShapeDtypeStruct((4, 2) + array.shape, BF16) for array in (packed, gate, up, down)
-    ]
-    return pl.pallas_call(
-        gather_kernel,
-        out_shape=shapes,
-        in_specs=[hbm] * 4,
-        out_specs=[hbm] * 4,
-        scratch_shapes=[
-            pltpu.SemaphoreType.DMA((4, N_PIECES)),
-            pltpu.SemaphoreType.DMA((4, N_PIECES)),
-            pltpu.SemaphoreType.DMA((4,)),
-        ],
-        name="gather_weights",
+    vmem = pl.BlockSpec(memory_space=pltpu.VMEM)
+    out = pl.pallas_call(
+        forward_kernel,
+        out_shape=[jax.ShapeDtypeStruct(*spec) for spec in FORWARD_OUTPUTS.values()],
+        in_specs=[hbm] * 4 + [vmem] * 7,
+        out_specs=[hbm] * 15 + [vmem],
+        scratch_shapes=list(forward_scratch().values()),
+        name="forward_pass",
         compiler_params=pltpu.CompilerParams(
-            collective_id=0, has_side_effects=True, vmem_limit_bytes=16 << 20
+            collective_id=0, has_side_effects=True, vmem_limit_bytes=60 << 20
         ),
-    )(packed, gate, up, down)
+    )(packed, gate, up, down, tokens, cotangent, mod, *tables)
+    return SimpleNamespace(**dict(zip(FORWARD_OUTPUTS, out)))
+
+
+def head_tables():
+    cosine, sine = rope_tables()
+
+    def lanes(table, signed):
+        first = -table if signed else table
+        return jnp.tile(jnp.stack([first, table], axis=2).reshape(SEQ, HD), (1, H))
+
+    head = jnp.arange(D) // HD
+    spread = (head[:, None] == jnp.arange(128)[None, :]).astype(BF16)
+    return lanes(cosine, False), lanes(sine, True), spread, spread.T
 
 
 SCATTER_ROWS = (144,) * 14 + (192,) * 3
 SCATTER_EDGE = tuple((32, 48)[j % 2] for j in range(14)) + (48,) * 3
-
-
-class Scatter:
-    def __init__(self, bufs, sems, outs, spot):
+ORDER = (14, 15, 16) + tuple(range(6, 14)) + tuple(range(6))
+
+
+class Reduce:
+    def __init__(self, s, spot):
+        self.s = s
         self.z, self.x, self.y, self.c = spot
-        self.held, self.got_y, self.got_x, self.got_z, self.mid, self.got_f, self.fin, self.got_c = bufs
-        self.send_sems, self.recv_sems = sems
-        self.outs = outs
+        self.stage = {}
+        self.open = []
 
     def shape(self, t):
         return SCATTER_ROWS[t], SCATTER_EDGE[t]
@@ -435,196 +876,655 @@
         rows, edge = self.shape(t)
         return pl.ds(pl.multiple_of(self.y * edge, 16), rows - edge)
 
-    def buf(self, group, t, rows=None):
-        big, small = group
-        return small.at[t] if t < 14 else big.at[t - 14]
+    def held(self, t):
+        s = self.s
+        return s.held_big.at[t - 14] if t >= 14 else s.held.at[t if t < 6 else t - 6]
+
+    def pick(self, small, big, t):
+        return big.at[t - 14] if t >= 14 else small.at[t]
+
+    def got_y(self, t):
+        return self.pick(self.s.got_y, self.s.got_y_big, t)
+
+    def got_x(self, t):
+        return self.pick(self.s.got_x, self.s.got_x_big, t)
+
+    def got_z(self, t):
+        return self.pick(self.s.got_z, self.s.got_z_big, t)
+
+    def got_f(self, t):
+        return self.pick(self.s.got_f, self.s.got_f_big, t)
+
+    def sems(self, stage, t):
+        return self.s.scatter_send.at[stage, t], self.s.scatter_recv.at[stage, t]
+
+    def produced(self, t):
+        self.stage[t] = -1
+        self.ask()
+
+    def ask(self):
+        entered = sum(stage > 0 for stage in self.stage.values())
+        for t in ORDER[: entered + 3]:
+            if self.stage.get(t) == -1:
+                self.stage[t] = 0
+                self.start_y(t)
+
+    def advance(self):
+        stages = (self.start_x, self.start_z, self.start_f, self.start_c)
+        under_way = [t for t in ORDER if 0 < self.stage.get(t, 4) < 4]
+        waiting = [t for t in ORDER if self.stage.get(t) == 0]
+        for t in under_way + waiting[:1]:
+            stages[self.stage[t]](t)
+            self.stage[t] += 1
+        self.ask()
+
+    def free(self, t):
+        while self.stage[t] < 4:
+            self.advance()
+        if t in self.open:
+            self.sent(t)
 
     def start_y(self, t):
         rows, edge = self.shape(t)
         theirs = pl.ds(pl.multiple_of((1 - self.y) * (rows - edge), 16), edge)
-        peer = device(self.z, self.x, 1 - self.y, self.c)
         send(
-            self.buf(self.held, t).at[:, :, theirs, :],
-            self.buf(self.got_y, t).at[:, :, pl.ds(0, edge), :],
-            self.send_sems.at[0, t],
-            self.recv_sems.at[0, t],
-            peer,
+            self.held(t).at[:, :, theirs, :],
+            self.got_y(t).at[:, :, pl.ds(0, edge), :],
+            *self.sems(0, t),
+            device(self.z, self.x, 1 - self.y, self.c),
         )
 
     def start_x(self, t):
         rows, edge = self.shape(t)
-        held = self.buf(self.held, t)
-        got = self.buf(self.got_y, t)
-        drain(got.at[:, :, pl.ds(0, edge), :], self.recv_sems.at[0, t])
+        held, got = self.held(t), self.got_y(t)
+        drain(got.at[:, :, pl.ds(0, edge), :], self.s.scatter_recv.at[0, t])
         mine = pl.ds(pl.multiple_of(self.y * (rows - edge), 16), edge)
 
-        for k in range(4):
+        @pl.loop(0, 4)
+        def _(k):
             for x in range(2):
-                total = held[k, x, mine, :].astype(F32) + got[k, x, :edge, :].astype(F32)
+                total = held[k, x, mine, :].astype(F32) + got[k, x, pl.ds(0, edge), :].astype(F32)
                 held[k, x, mine, :] = total.astype(BF16)
-        peer = device(self.z, 1 - self.x, self.y, self.c)
+
         send(
             held.at[:, 1 - self.x, self.part(t), :],
-            self.buf(self.got_x, t).at[:, pl.ds(0, rows - edge), :],
-            self.send_sems.at[1, t],
-            self.recv_sems.at[1, t],
-            peer,
+            self.got_x(t).at[:, pl.ds(0, rows - edge), :],
+            *self.sems(1, t),
+            device(self.z, 1 - self.x, self.y, self.c),
         )
 
     def start_z(self, t):
         rows, edge = self.shape(t)
-        held = self.buf(self.held, t)
-        got = self.buf(self.got_x, t)
-        drain(got.at[:, pl.ds(0, rows - edge), :], self.recv_sems.at[1, t])
+        held, got = self.held(t), self.got_x(t)
+        keep = rows - edge
+        drain(got.at[:, pl.ds(0, keep), :], self.s.scatter_recv.at[1, t])
         part = self.part(t)
-        for k in range(4):
-            total = held[k, self.x, part, :].astype(F32) + got[k, : rows - edge, :].astype(F32)
+
+        @pl.loop(0, 4)
+        def _(k):
+            total = held[k, self.x, part, :].astype(F32) + got[k, pl.ds(0, keep), :].astype(F32)
             held[k, self.x, part, :] = total.astype(BF16)
+
         for step in (1, 3, 2):
             other = (self.z + step) % 4
             send(
                 held.at[other, self.x, part, :],
-                self.buf(self.got_z, t).at[step - 1, pl.ds(0, rows - edge), :],
-                self.send_sems.at[2, t],
-                self.recv_sems.at[2, t],
+                self.got_z(t).at[step - 1, pl.ds(0, keep), :],
+                *self.sems(2, t),
                 device(other, self.x, self.y, self.c),
             )
 
     def start_f(self, t):
         rows, edge = self.shape(t)
-        held = self.buf(self.held, t)
-        got = self.buf(self.got_z, t)
-        drain(got.at[:, pl.ds(0, rows - edge), :], self.recv_sems.at[2, t])
-        total = held[self.z, self.x, self.part(t), :].astype(F32)
+        held, got = self.held(t), self.got_z(t)
+        keep = rows - edge
+        drain(got.at[:, pl.ds(0, keep), :], self.s.scatter_recv.at[2, t])
+        part = self.part(t)
+        total = held[self.z, self.x, part, :].astype(F32)
         for k in range(3):
-            total = total + got[k, : rows - edge, :].astype(F32)
-        mid = self.buf(self.mid, t)
-        mid[: rows - edge, :] = total.astype(BF16)
+            total = total + got[k, pl.ds(0, keep), :].astype(F32)
+        held[self.z, self.x, part, :] = total.astype(BF16)
         send(
-            mid.at[pl.ds(0, rows - edge), :],
-            self.buf(self.got_f, t).at[pl.ds(0, rows - edge), :],
-            self.send_sems.at[3, t],
-            self.recv_sems.at[3, t],
+            held.at[self.z, self.x, part, :],
+            self.got_f(t).at[pl.ds(0, keep), :],
+            *self.sems(3, t),
             device(self.z, self.x, 1 - self.y, self.c),
         )
 
+    def target(self, t):
+        s = self.s
+        if t < 6:
+            columns = pl.ds(pl.multiple_of(self.c * LANE_HALF + t * WIDTH, 128), WIDTH)
+            return s.g_packed.at[:, columns]
+        if t < 14:
+            columns = pl.ds(pl.multiple_of(self.c * FF_HALF + (t - 6) // 2 * WIDTH, 128), WIDTH)
+            return (s.g_gate, s.g_up)[(t - 6) % 2].at[:, columns]
+        rows = pl.ds(pl.multiple_of(self.c * 192, 16), 192)
+        return s.g_down.at[rows, pl.ds((t - 14) * WIDTH, WIDTH)]
+
     def start_c(self, t):
         rows, edge = self.shape(t)
-        mid, got, fin = self.buf(self.mid, t), self.buf(self.got_f, t), self.buf(self.fin, t)
-        y = self.y
-        drain(got.at[pl.ds(0, rows - edge), :], self.recv_sems.at[3, t])
-        both = rows - 2 * edge
+        held, got = self.held(t), self.got_f(t)
+        y, keep, both = self.y, rows - edge, rows - 2 * edge
+        drain(got.at[pl.ds(0, keep), :], self.s.scatter_recv.at[3, t])
+        drain(self.got_y(t).at[:, :, pl.ds(0, edge), :], self.s.scatter_send.at[0, t])
+        drain(self.got_x(t).at[:, pl.ds(0, keep), :], self.s.scatter_send.at[1, t])
+        mid, fin = held.at[self.z, self.x], held.at[self.z, 1 - self.x]
 
         def at(offset, count):
             return pl.ds(pl.multiple_of(offset, 16), count)
 
-        fin[at(y * (rows - edge), edge), :] = mid[at(y * both, edge), :]
-        fin[at((1 - y) * (rows - edge), edge), :] = got[at((1 - y) * both, edge), :]
-        total = mid[at((1 - y) * edge, both), :].astype(F32) + got[at(y * edge, both), :].astype(F32)
-        fin[edge : edge + both, :] = total.astype(BF16)
-        send(
-            fin,
-            self.buf(self.got_c, t),
-            self.send_sems.at[4, t],
-            self.recv_sems.at[4, t],
-            device(self.z, self.x, self.y, 1 - self.c),
+        own, other = at(y * keep, edge), at((1 - y) * keep, edge)
+        fin[own, :] = mid[own, :]
+        fin[other, :] = got[at((1 - y) * both, edge), :]
+        total = mid[pl.ds(edge, both), :].astype(F32) + got[at(y * edge, both), :].astype(F32)
+        fin[pl.ds(edge, both), :] = total.astype(BF16)
+        target = self.target(t)
+        send(fin, target, *self.sems(4, t), device(self.z, self.x, y, 1 - self.c))
+        pltpu.make_async_copy(fin, target, self.s.store_sems.at[t]).start()
+        self.open.append(t)
+
+    def sent(self, t):
+        self.open.remove(t)
+        rows, edge = self.shape(t)
+        sems = self.s.scatter_send
+        drain(self.got_z(t).at[:, pl.ds(0, rows - edge), :], sems.at[2, t])
+        drain(self.got_f(t).at[pl.ds(0, rows - edge), :], sems.at[3, t])
+        drain(self.target(t), sems.at[4, t])
+        drain(self.target(t), self.s.store_sems.at[t])
+
+    def finish(self):
+        for t in ORDER:
+            self.free(t)
+        for t in range(N_PIECES):
+            drain(self.target(t), self.s.scatter_recv.at[4, t])
+
+
+class Backward:
+    def __init__(self, s, spot, reduce):
+        self.s, self.reduce = s, reduce
+        self.z, self.x, self.y, self.c = spot
+        self.pending = {}
+        self.remote = {}
+        self.copies = 0
+
+    def load(self, key, source, target):
+        if key not in self.pending:
+            copy = pltpu.make_async_copy(source, target, self.s.load_sems.at[self.copies])
+            self.copies += 1
+            copy.start()
+            self.pending[key] = copy
+
+    def wait(self, *keys):
+        for key in keys:
+            self.pending.pop(key).wait()
+
+    def to_sibling(self, key, source, target):
+        k = len(self.remote)
+        copy = pltpu.make_async_remote_copy(
+            src_ref=source,
+            dst_ref=target,
+            send_sem=self.s.pair_send.at[k],
+            recv_sem=self.s.pair_recv.at[k],
+            device_id=device(self.z, self.x, self.y, 1 - self.c),
+            device_id_type=MESH,
         )
-        self.store(t, fin, self.c)
-
-    def finish(self, t):
-        got = self.buf(self.got_c, t)
-        drain(got, self.recv_sems.at[4, t])
-        self.store(t, got, 1 - self.c)
-
-    def store(self, t, block, core):
-        packed, gate, up, down = self.outs
-        if t < 6:
-            columns = pl.ds(pl.multiple_of(core * LANE_HALF + t * WIDTH, 128), WIDTH)
-            packed[:, columns] = block[...].astype(F32)
-        elif t < 14:
-            target = (gate, up)[(t - 6) % 2]
-            columns = pl.ds(pl.multiple_of(core * FF_HALF + (t - 6) // 2 * WIDTH, 128), WIDTH)
-            target[:, columns] = block[...].astype(F32)
+        copy.start()
+        self.remote[key] = copy
+
+
+    def grad_down(self, hidden, branch):
+        s, reduce = self.s, self.reduce
+
+        @pl.loop(0, 4)
+        def _(k):
+            left = hidden[pl.ds(2 * k, 2)].reshape(384, 2 * TOK)
+            total = mm(left, branch[...]).astype(BF16)
+            for j in range(3):
+                block = total[:, j * WIDTH : (j + 1) * WIDTH]
+                s.held_big[j, k] = block.reshape(2, 192, WIDTH)
+
+        for t in (14, 15, 16):
+            reduce.produced(t)
+
+    def column(self, w):
+        half = (1 - self.c) if w % 2 == 0 else self.c
+        return half * 4 + w // 2
+
+    def load_ff(self, f, w):
+        s = self.s
+        window = self.column(w)
+        columns = pl.ds(pl.multiple_of(window * WIDTH, 128), WIDTH)
+        slot = w % 2
+        self.load((1, w), s.down_all.at[window // 2, window % 2], f.w_down.at[slot])
+        self.load((2, w), s.gate_all.at[:, :, :, columns], s.w.at[slot, :, :, :, pl.ds(0, WIDTH)])
+        self.load((3, w), s.up_all.at[:, :, :, columns], s.w.at[slot, :, :, :, pl.ds(WIDTH, WIDTH)])
+        self.load((4, w), s.o_active.at[window], f.active.at[slot])
+
+    def ff(self, f, w):
+        s = self.s
+        slot = w % 2
+        self.load_ff(f, w)
+        self.wait((1, w), (2, w), (3, w), (4, w))
+        if w < 7:
+            self.load_ff(f, w + 1)
+        f.wide[...] = mm_nt(f.branch[pl.ds(0, TOK), :], f.w_down[slot])
+        if w >= 2:
+            if slot == 0:
+                self.remote[5, w - 2].wait_send()
+            else:
+                self.wait((5, w - 2))
+        steep = f.steep.at[slot]
+
+        @pl.loop(0, TOK // TILE)
+        def _(i):
+            rows = rows_of(i, TILE)
+            back = f.wide[rows, :]
+            steep[rows, 0:WIDTH] = (back * f.active[slot, 1, rows, :].astype(F32)).astype(BF16)
+            steep[rows, WIDTH : 2 * WIDTH] = (
+                back * f.active[slot, 0, rows, :].astype(F32)
+            ).astype(BF16)
+
+        j = w // 2
+        if slot == 0:
+            self.to_sibling((5, w), steep, s.r_ff.at[j, pl.ds(TOK, TOK)])
         else:
-            rows = pl.ds(pl.multiple_of(core * 192, 16), 192)
-            down[rows, (t - 14) * WIDTH : (t - 13) * WIDTH] = block[...].astype(F32)
-
-    def sent(self, t):
-        rows, edge = self.shape(t)
-        drain(self.buf(self.got_y, t).at[:, :, pl.ds(0, edge), :], self.send_sems.at[0, t])
-        drain(self.buf(self.got_x, t).at[:, pl.ds(0, rows - edge), :], self.send_sems.at[1, t])
-        drain(self.buf(self.got_z, t).at[:, pl.ds(0, rows - edge), :], self.send_sems.at[2, t])
-        drain(self.buf(self.got_f, t).at[pl.ds(0, rows - edge), :], self.send_sems.at[3, t])
-        drain(self.buf(self.got_c, t), self.send_sems.at[4, t])
-
-
-def scatter_scratch():
-    shapes = []
-    for lead, share in (((4, 2), 1), ((4, 2), 3), ((4,), 2), ((3,), 2), ((), 2), ((), 2), ((), 1), ((), 1)):
-        for count, rows, edges in ((3, 192, (48, 48)), (14, 144, (32, 48))):
-            height = {1: rows, 3: max(edges), 2: rows - min(edges)}[share]
-            shapes.append(pltpu.VMEM((count,) + lead + (height, WIDTH), BF16))
-    return shapes
-
-
-def scatter_kernel(half_packed, half_gate, half_up, half_down, *rest):
-    outs = rest[:4]
-    scratch = rest[4:20]
-    send_sems, recv_sems, load_sems = rest[20:]
-    bufs = [(scratch[2 * k], scratch[2 * k + 1]) for k in range(8)]
+            self.load((5, w), steep, s.r_ff.at[j, pl.ds(0, TOK)])
+        product = mm_nt(steep[...], flat(s.w[slot]))
+        if w == 0:
+            s.acc[...] = product
+        else:
+            s.acc[...] += product
+
+    def load_grad_ff(self, j):
+        s = self.s
+        self.remote[5, 2 * j].wait_recv()
+        if (5, 2 * j + 1) in self.pending:
+            self.wait((5, 2 * j + 1))
+        self.load((6, j), s.r_ff.at[j], s.right.at[j % 2])
+
+    def grad_ff(self, j):
+        s = self.s
+        self.wait((6, j))
+        right = s.right.at[j % 2]
+
+        @pl.loop(0, 4)
+        def _(k):
+            left = s.left[pl.ds(pl.multiple_of(k * 288, 32), 288), :]
+            total = mm(left, right[...]).astype(BF16)
+            for half in range(2):
+                block = total[:, half * WIDTH : (half + 1) * WIDTH]
+                s.held[2 * j + half, k] = block.reshape(2, 144, WIDTH)
+
+        self.reduce.produced(6 + 2 * j)
+        self.reduce.produced(7 + 2 * j)
+
+    def feed_forward(self, f):
+        s, reduce = self.s, self.reduce
+        self.wait(11, 12)
+        self.load((7, 0), s.o_lhs.at[2], s.left)
+        self.grad_down(f.hidden, f.branch)
+        for w in range(8):
+            self.ff(f, w)
+            if w == 0:
+                self.wait((7, 0))
+            if w % 2 == 1:
+                reduce.advance()
+                if w >= 3:
+                    self.load_grad_ff(w // 2 - 1)
+            elif w >= 4:
+                self.grad_ff(w // 2 - 2)
+        self.load_grad_ff(3)
+        self.grad_ff(2)
+        reduce.advance()
+        self.grad_ff(3)
+        self.remote[5, 6].wait_send()
+
+
+    def middle(self, f):
+        s = self.s
+        self.load(21, s.cot, f.cot)
+        self.load(22, s.o_residual, s.d_residual)
+        self.load(23, s.o_attended, f.attended)
+        self.wait(21, 22, 23)
+        s.d_mod[...] = jnp.zeros_like(s.d_mod)
+
+        @pl.loop(0, TOK // TILE)
+        def _(i):
+            rows = rows_of(i, TILE)
+            image = i // (SEQ // TILE)
+            mod, d_mod = s.mod, s.d_mod
+            normed, inverse = norm_rows(s.d_residual[rows, :])
+            d_entry = s.acc[rows, :]
+            d_mod[image, 3:4, :] += jnp.sum(d_entry, axis=0, keepdims=True)
+            d_mod[image, 4:5, :] += jnp.sum(d_entry * normed, axis=0, keepdims=True)
+            back = norm_back(normed, inverse, d_entry * (1.0 + mod[image, 4:5, :]))
+            d_residual = f.cot[rows, :].astype(F32) + back
+            s.d_residual[rows, :] = d_residual
+            attended = f.attended[rows, :].astype(F32)
+            d_mod[image, 2:3, :] += jnp.sum(d_residual * attended, axis=0, keepdims=True)
+            s.joined[rows, 3 * D : 4 * D] = (mod[image, 2:3, :] * d_residual).astype(BF16)
+
+
+    def load_soft(self, f, k):
+        heads = H // ATTN_STEPS
+        self.load((31, k), self.s.o_soft.at[pl.ds(k * heads, heads)], f.soft.at[k % 2])
+
+    def attend(self, f, k):
+        s = self.s
+        heads = H // ATTN_STEPS
+        self.load_soft(f, k)
+        self.wait((31, k))
+        if k + 1 < ATTN_STEPS:
+            self.load_soft(f, k + 1)
+        factor = 1.0 / math.sqrt(HD)
+
+        @pl.loop(0, heads)
+        def _(i):
+            head = k * heads + i
+            window, mask = head_window(head)
+            base = jnp.minimum(head * HD // 128 * 128, D - 256)
+            for image in range(2):
+                rows = pl.ds(image * SEQ, SEQ)
+                back = jnp.where(mask, f.back[rows, window].astype(F32), 0.0).astype(BF16)
+                soft = f.soft[k % 2, i, image]
+                d_soft = mm_nt(back, f.qkv[2, rows, window])
+                wide = soft.astype(F32)
+                d_scores = (
+                    wide * (d_soft - jnp.sum(wide * d_soft, axis=1, keepdims=True))
+                ).astype(BF16)
+                results = (
+                    mm(d_scores, f.qkv[1, rows, window]) * factor,
+                    mm_tn(d_scores, f.qkv[0, rows, window]) * factor,
+                    mm_tn(soft, back),
+                )
+                for part, result in enumerate(results):
+                    place_at = pl.ds(pl.multiple_of(part * D + base, 128), 256)
+                    old = s.joined[rows, place_at].astype(F32)
+                    s.joined[rows, place_at] = jnp.where(mask, result, old).astype(BF16)
+
+    def head_back(self, f, which):
+        s = self.s
+
+        @pl.loop(0, TOK // TILE)
+        def _(i):
+            rows = rows_of(i, TILE)
+            spots = rows_of(i % (SEQ // TILE), TILE)
+            columns = pl.ds(which * D, D)
+            grad = s.joined[rows, columns].astype(F32)
+            grad = grad * f.cos[spots, :] - partner(grad, first_lanes(TILE)) * f.sin[spots, :]
+            normed = f.normed[which, rows, :].astype(F32)
+            mean = mm_split(grad * normed, s.spread[...]) * (1.0 / HD)
+            scale = mm_split(f.scale[which, rows, :], s.widen[...])
+            result = scale * (grad - normed * mm_split(mean, s.widen[...]))
+            s.joined[rows, columns] = result.astype(BF16)
+
+    def attention(self, f):
+        s, reduce = self.s, self.reduce
+        self.load(24, s.packed_all.at[:, :, :, pl.ds(3 * D, 768)], s.w.at[0])
+        self.load(25, s.packed_all.at[:, :, :, pl.ds(3 * D + 768, WIDTH)], s.w.at[1, :, :, :, pl.ds(0, WIDTH)])
+        for k in range(3):
+            self.load((41, k), s.o_qkv.at[k], f.qkv.at[k])
+        self.load_soft(f, 0)
+        self.load(42, s.o_normed, f.normed)
+        self.load(43, s.o_scale, f.scale)
+        self.load(44, s.cos, f.cos)
+        self.load(45, s.sin, f.sin)
+        self.wait(24, 25)
+        joined = s.joined
+        s.acc[...] = mm_nt(joined[:, 3 * D : 3 * D + 768], flat(s.w[0]))
+        s.acc[...] += mm_nt(joined[:, 3 * D + 768 :], flat(s.w[1, :, :, :, 0:WIDTH]))
+        f.back[...] = s.acc[...].astype(BF16)
+        self.wait((41, 0), (41, 1), (41, 2))
+        for k in range(ATTN_STEPS):
+            self.attend(f, k)
+            reduce.advance()
+        self.wait(42, 43, 44, 45)
+        self.head_back(f, 0)
+        reduce.advance()
+        self.head_back(f, 1)
+
+
+    def load_entry(self, k):
+        s = self.s
+        width = 768 if k < 4 else WIDTH
+        self.load(
+            (51, k),
+            s.packed_all.at[:, :, :, pl.ds(k * 768, width)],
+            s.w.at[k % 2, :, :, :, pl.ds(0, width)],
+        )
+
+    def entry(self, k):
+        s = self.s
+        width = 768 if k < 4 else WIDTH
+        self.load_entry(k)
+        self.wait((51, k))
+        if k < 4:
+            self.load_entry(k + 1)
+        product = mm_nt(s.joined[:, k * 768 : k * 768 + width], flat(s.w[k % 2, :, :, :, 0:width]))
+        if k == 0:
+            s.acc[...] = product
+        else:
+            s.acc[...] += product
+
+    def grad_packed(self, f, jj):
+        s = self.s
+        self.wait((61, jj))
+        right = s.right.at[jj % 2]
+
+        @pl.loop(0, 4)
+        def _(k):
+            rows = pl.ds(pl.multiple_of(k * 288, 32), 288)
+            for half in range(2):
+                j = 2 * jj + half
+                left = s.left if j < 3 else f.left
+                total = mm(left[rows, :], right[:, half * WIDTH : (half + 1) * WIDTH])
+                s.held[j, k] = total.astype(BF16).reshape(2, 144, WIDTH)
+
+        self.reduce.produced(2 * jj)
+        self.reduce.produced(2 * jj + 1)
+
+    def load_right(self, jj):
+        self.load((61, jj), self.s.r_packed.at[:, pl.ds(768 * jj, 768)], self.s.right.at[jj % 2])
+
+    def last(self, f):
+        s, reduce = self.s, self.reduce
+        mine = pl.ds(pl.multiple_of(self.c * LANE_HALF, 128), LANE_HALF)
+        theirs = pl.ds(pl.multiple_of((1 - self.c) * LANE_HALF, 128), LANE_HALF)
+        self.to_sibling((71, 0), s.joined.at[:, theirs], s.r_packed.at[pl.ds(TOK, TOK)])
+        self.load(71, s.joined.at[:, mine], s.r_packed.at[pl.ds(0, TOK)])
+        self.load(72, s.o_lhs.at[0], s.left)
+        self.load(73, s.o_lhs.at[self.c], f.left)
+        self.load(74, s.tokens, f.tokens)
+        reduce.advance()
+        self.entry(0)
+        self.remote[71, 0].wait_recv()
+        self.wait(71, 72, 73)
+        self.load_right(0)
+        self.load_right(1)
+        for jj in range(3):
+            reduce.free(6 + 2 * jj)
+            reduce.free(7 + 2 * jj)
+            self.grad_packed(f, jj)
+            if jj == 0:
+                self.load_right(2)
+            self.entry(1 + jj)
+            reduce.advance()
+        self.entry(4)
+        reduce.advance()
+        self.wait(74)
+
+        @pl.loop(0, TOK // TILE)
+        def _(i):
+            rows = rows_of(i, TILE)
+            image = i // (SEQ // TILE)
+            mod, d_mod = s.mod, s.d_mod
+            normed, inverse = norm_rows(f.tokens[rows, :].astype(F32))
+            d_entry = s.acc[rows, :]
+            d_mod[image, 0:1, :] += jnp.sum(d_entry, axis=0, keepdims=True)
+            d_mod[image, 1:2, :] += jnp.sum(d_entry * normed, axis=0, keepdims=True)
+            back = norm_back(normed, inverse, d_entry * (1.0 + mod[image, 1:2, :]))
+            s.d_residual[rows, :] += back
+
+        self.load(75, s.d_residual, s.g_tokens)
+        reduce.finish()
+        self.wait(75)
+        self.remote[71, 0].wait_send()
+
+
+class BackwardInputs(NamedTuple):
+    packed_all: object
+    gate_all: object
+    up_all: object
+    down_all: object
+    o_branch: object
+    o_lhs: object
+    o_hidden: object
+    o_qkv: object
+    o_normed: object
+    o_scale: object
+    o_soft: object
+    o_attended: object
+    o_residual: object
+    o_active: object
+    tokens: object
+    cot: object
+    cos: object
+    sin: object
+    mod: object
+    spread: object
+    widen: object
+
+
+BACKWARD_OUTPUTS = dict(
+    g_packed=((144, 4 * D), BF16),
+    g_gate=((144, 8 * WIDTH), BF16),
+    g_up=((144, 8 * WIDTH), BF16),
+    g_down=((384, D), BF16),
+    g_tokens=((TOK, D), F32),
+    r_ff=((4, 2 * TOK, 2 * WIDTH), BF16),
+    r_packed=((2 * TOK, LANE_HALF), BF16),
+    d_mod=((2, 8, D), F32),
+)
+
+
+def vmem(*shape, kind=BF16):
+    return pltpu.VMEM(shape, kind)
+
+
+def backward_scratch():
+    return dict(
+        held=vmem(8, 4, 2, 144, WIDTH),
+        held_big=vmem(3, 4, 2, 192, WIDTH),
+        got_y=vmem(14, 4, 2, 48, WIDTH),
+        got_y_big=vmem(3, 4, 2, 48, WIDTH),
+        got_x=vmem(14, 4, 112, WIDTH),
+        got_x_big=vmem(3, 4, 144, WIDTH),
+        got_z=vmem(14, 3, 112, WIDTH),
+        got_z_big=vmem(3, 3, 144, WIDTH),
+        got_f=vmem(14, 112, WIDTH),
+        got_f_big=vmem(3, 144, WIDTH),
+        w=vmem(2, 4, 2, 144, 2 * WIDTH),
+        acc=vmem(TOK, D, kind=F32),
+        d_residual=vmem(TOK, D, kind=F32),
+        joined=vmem(TOK, 4 * D),
+        left=vmem(D, 2 * TOK),
+        right=vmem(2, 2 * TOK, 2 * WIDTH),
+        scatter_send=pltpu.SemaphoreType.DMA((5, N_PIECES)),
+        scatter_recv=pltpu.SemaphoreType.DMA((5, N_PIECES)),
+        store_sems=pltpu.SemaphoreType.DMA((N_PIECES,)),
+        load_sems=pltpu.SemaphoreType.DMA((96,)),
+        pair_send=pltpu.SemaphoreType.DMA((8,)),
+        pair_recv=pltpu.SemaphoreType.DMA((8,)),
+    )
+
+
+def backward_kernel(*refs):
+    names = BackwardInputs._fields + tuple(BACKWARD_OUTPUTS) + tuple(backward_scratch())
+    s = SimpleNamespace(**dict(zip(names, refs, strict=True)))
     spot = place()
     greet(neighbours(*spot))
-    scatter = Scatter(bufs, (send_sems, recv_sems), outs, spot)
-    order = list(range(14, 17)) + list(range(6, 14)) + list(range(6))
-    loads = []
-    for t in range(N_PIECES):
-        if t < 6:
-            source = half_packed.at[:, :, :, pl.ds(t * WIDTH, WIDTH)]
-        elif t < 14:
-            source = (half_gate, half_up)[(t - 6) % 2].at[:, :, :, pl.ds((t - 6) // 2 * WIDTH, WIDTH)]
-        else:
-            source = half_down.at[:, :, :, pl.ds((t - 14) * WIDTH, WIDTH)]
-        loads.append(pltpu.make_async_copy(source, scatter.buf(scatter.held, t), load_sems.at[t]))
-    for t in order:
-        loads[t].start()
-    ahead = 2
-    for k in range(N_PIECES + 6 + ahead):
-        if k < N_PIECES:
-            loads[order[k]].wait()
-            scatter.start_y(order[k])
-        for lag, stage in enumerate(
-            (scatter.start_x, scatter.start_z, scatter.start_f, scatter.start_c, scatter.finish)
-        ):
-            if 0 <= k - ahead - lag < N_PIECES:
-                stage(order[k - ahead - lag])
-    for t in range(N_PIECES):
-        scatter.sent(t)
-
-
-def scatter_grads(half_packed, half_gate, half_up, half_down):
+    reduce = Reduce(s, spot)
+    work = Backward(s, spot, reduce)
+
+    def scoped(act, before=None, **shapes):
+        def run(*held):
+            f = SimpleNamespace(**dict(zip(shapes, held, strict=True)))
+            if before is not None:
+                before(f)
+            act(f)
+
+        pl.run_scoped(run, *shapes.values())
+
+    def first_loads(f):
+        work.load(11, s.o_hidden, f.hidden)
+        work.load(12, s.o_branch, f.branch)
+        work.load_ff(f, 0)
+
+    scoped(
+        work.feed_forward,
+        first_loads,
+        hidden=vmem(8, 192, 2 * TOK),
+        branch=vmem(2 * TOK, D),
+        w_down=vmem(2, 384, D),
+        active=vmem(2, 2, TOK, WIDTH),
+        wide=vmem(TOK, WIDTH, kind=F32),
+        steep=vmem(2, TOK, 2 * WIDTH),
+    )
+    scoped(work.middle, cot=vmem(TOK, D), attended=vmem(TOK, D))
+    reduce.advance()
+    scoped(
+        work.attention,
+        qkv=vmem(3, TOK, D),
+        normed=vmem(2, TOK, D),
+        scale=vmem(2, TOK, 128, kind=F32),
+        soft=vmem(2, H // ATTN_STEPS, 2, SEQ, SEQ),
+        back=vmem(TOK, D),
+        cos=vmem(SEQ, D, kind=F32),
+        sin=vmem(SEQ, D, kind=F32),
+    )
+    scoped(work.last, left=vmem(D, 2 * TOK), tokens=vmem(TOK, D))
+
+
+def backward_pass(f, tokens, cotangent, mod, tables):
     hbm = pl.BlockSpec(memory_space=pl.ANY)
-    vmem = pl.BlockSpec(memory_space=pltpu.VMEM)
-    return pl.pallas_call(
-        scatter_kernel,
-        out_shape=[
-            jax.ShapeDtypeStruct((144, 4608), F32),
-            jax.ShapeDtypeStruct((144, 3072), F32),
-            jax.ShapeDtypeStruct((144, 3072), F32),
-            jax.ShapeDtypeStruct((384, 1152), F32),
-        ],
-        in_specs=[hbm] * 4,
-        out_specs=[vmem] * 4,
-        scratch_shapes=scatter_scratch()
-        + [
-            pltpu.SemaphoreType.DMA((5, N_PIECES)),
-            pltpu.SemaphoreType.DMA((5, N_PIECES)),
-            pltpu.SemaphoreType.DMA((N_PIECES,)),
-        ],
-        name="scatter_grads",
+    inside = pl.BlockSpec(memory_space=pltpu.VMEM)
+    cosine, sine, spread, widen = tables
+    given = BackwardInputs(
+        f.packed_all,
+        f.gate_all,
+        f.up_all,
+        f.down_all,
+        f.o_branch,
+        f.o_lhs,
+        f.o_hidden,
+        f.o_qkv,
+        f.o_normed,
+        f.o_scale,
+        f.o_soft,
+        f.o_attended,
+        f.o_residual,
+        f.o_active,
+        tokens,
+        cotangent,
+        cosine,
+        sine,
+        mod,
+        spread,
+        widen,
+    )
+    out = pl.pallas_call(
+        backward_kernel,
+        out_shape=[jax.ShapeDtypeStruct(*spec) for spec in BACKWARD_OUTPUTS.values()],
+        in_specs=[hbm] * 18 + [inside] * 3,
+        out_specs=[hbm] * 7 + [inside],
+        scratch_shapes=list(backward_scratch().values()),
+        name="backward_pass",
         compiler_params=pltpu.CompilerParams(
             collective_id=1, has_side_effects=True, vmem_limit_bytes=60 << 20
         ),
-    )(half_packed, half_gate, half_up, half_down)
+    )(*given)
+    return SimpleNamespace(**dict(zip(BACKWARD_OUTPUTS, out)))
 
 
 def body_general(
@@ -742,10 +1642,6 @@
     )
 
 
-def pair_exchange(array):
-    return lax.ppermute(array, "mod", [(0, 1), (1, 0), (2, 3), (3, 2)])
-
-
 def body_fast(
     tokens,
     condition,
@@ -759,19 +1655,7 @@
     mod_bias,
     cotangent,
 ):
-    core = lax.axis_index("mod") % 2
     packed = jnp.concatenate([qkv_weight, out_weight], axis=1)
-    packed_all, gate_all, up_all, down_all = gather_weights(
-        packed, gate_weight, up_weight, down_weight
-    )
-    packed_all = packed_all.reshape(D, 4 * D)
-    gathered = (
-        packed_all[:, : 3 * D],
-        packed_all[:, 3 * D :],
-        gate_all.reshape(D, -1),
-        up_all.reshape(D, -1),
-        down_all.reshape(-1, D),
-    )
     cond_total = condition.astype(jnp.float32) + embed_steps(timestep)
     acted_cond = jax.nn.silu(cond_total).astype(jnp.bfloat16)
     acted_group = lax.all_gather(acted_cond, "mod", axis=0, tiled=True)
@@ -782,58 +1666,21 @@
     modulation = lax.all_to_all(mod_part, "mod", split_axis=0, concat_axis=1, tiled=True).astype(
         jnp.float32
     )
-    tables = rope_tables()
-    output_tokens, grad_tokens, mod_grad, factors = layer_pass(
-        tokens, modulation, cotangent, gathered, tables
-    )
-    (
-        entry_first,
-        d_projected,
-        combined,
-        d_attended,
-        entry_second,
-        d_gate_proj,
-        d_up_proj,
-        hidden,
-        d_branch,
-    ) = [factor.reshape(-1, factor.shape[-1]) for factor in factors]
-
-    def pair(factor):
-        return jnp.concatenate([factor, pair_exchange(factor)], axis=0)
-
-    def half(factor, width):
-        return lax.dynamic_slice_in_dim(factor, core * width, width, 1)
-
-    def other(factor, width):
-        return lax.dynamic_slice_in_dim(factor, (1 - core) * width, width, 1)
-
-    def pair_half(factor, width):
-        return jnp.concatenate(
-            [half(factor, width), pair_exchange(other(factor, width))], axis=0
-        )
-
-    def outer(left, right):
-        return lax.dot_general(
-            left, right, (((0,), (0,)), ((), ())), preferred_element_type=jnp.float32
-        ).astype(BF16)
-
-    entry_pair = pair(entry_first)
-    second_pair = jnp.where(core == 0, entry_pair, pair(combined))
-    packed_pair = pair_half(jnp.concatenate([d_projected, d_attended], axis=1), LANE_HALF)
-    half_packed = jnp.concatenate(
-        [outer(entry_pair, packed_pair[:, :D]), outer(second_pair, packed_pair[:, D:])], axis=1
-    )
-    entry_pair_b = pair(entry_second)
-    half_gate = outer(entry_pair_b, pair_half(d_gate_proj, FF_HALF))
-    half_up = outer(entry_pair_b, pair_half(d_up_proj, FF_HALF))
-    by_core = hidden.reshape(-1, 8, 2, 192).transpose(0, 2, 1, 3).reshape(-1, 2 * FF_HALF)
-    half_down = outer(pair_half(by_core, FF_HALF), pair(d_branch))
-    grads = scatter_grads(
-        half_packed.reshape(4, 2, 144, -1),
-        half_gate.reshape(4, 2, 144, -1),
-        half_up.reshape(4, 2, 144, -1),
-        half_down.reshape(4, 2, 192, -1),
-    )
+    mod_rows = jnp.pad(modulation.reshape(2, 6, D), ((0, 0), (0, 2), (0, 0)))
+    flat_tokens, flat_cotangent = tokens.reshape(TOK, D), cotangent.reshape(TOK, D)
+    tables = head_tables()
+    f = forward_pass(
+        packed,
+        gate_weight,
+        up_weight,
+        down_weight,
+        flat_tokens,
+        flat_cotangent,
+        mod_rows,
+        tables,
+    )
+    b = backward_pass(f, flat_tokens, flat_cotangent, mod_rows, tables)
+    mod_grad = b.d_mod[:, :6, :].at[:, 5, :].set(f.o_gate_b[:, 0, :]).reshape(2, 6 * D).astype(BF16)
     mod_back = lax.all_to_all(mod_grad, "mod", split_axis=1, concat_axis=0, tiled=True)
     acted_all = lax.all_gather(acted_group, "dp", axis=0, tiled=True)
     back_all = lax.all_gather(mod_back, "dp", axis=0, tiled=True)
@@ -850,14 +1697,14 @@
     sigma_cond = jax.nn.sigmoid(cond_total)
     grad_condition = acted_grad * sigma_cond * (1.0 + cond_total * (1.0 - sigma_cond))
     return (
-        output_tokens,
-        grad_tokens,
+        f.o_result.reshape(tokens.shape),
+        b.g_tokens.reshape(tokens.shape),
         grad_condition,
-        grads[0][:, : 3 * D],
-        grads[0][:, 3 * D :],
-        grads[1],
-        grads[2],
-        grads[3],
+        b.g_packed[:, : 3 * D].astype(F32),
+        b.g_packed[:, 3 * D :].astype(F32),
+        b.g_gate.astype(F32),
+        b.g_up.astype(F32),
+        b.g_down.astype(F32),
         grad_mod,
         grad_bias,
     )

time: 750 us -> 501 us (0.67); the launches traced: 739 us -> 497 us
  matrix products: 146 us -> 7.48 us
  local copies, waits for them, and re-layouts: 143 us -> 10.8 us
  Pallas kernels: 293 us -> 376 us
  other arithmetic: 62 us -> 16.1 us
    dot_general x21 -> x0, matrix products: 138 us -> none  [the longest x5 33.9 us: outer(): lax.dot_general(left, right, (((0,), (0,)), ((), ())), preferred_element_...]
    pallas_call x2, Pallas kernels: 293 us -> 376 us  [the longest x1 221 us: backward_pass(): pl.pallas_call(backward_kernel, out_shape=[jax.ShapeDtypeStruct(*spec) fo...]
    unnamed x176 -> x20, local copies, waits for them, and re-layouts: 38.4 us -> 4.41 us
    mul x10 -> x0, local copies, waits for them, and re-layouts: 25.6 us -> none  [the longest x4 10.9 us: norm_rows(): return (field * scale_inv, scale_inv)]
    reshape x7 -> x0, local copies, waits for them, and re-layouts: 17.5 us -> none  [the longest x2 10 us: rotate(): jnp.stack([turned_first, turned_second], axis=-2).reshape(field.shape)]
    slice x8 -> x2, local copies, waits for them, and re-layouts: 18.4 us -> 1.86 us  [the longest x1 0.97 us: body_fast(): b.d_mod[:, :6, :].at[:, 5, :].set(f.o_gate_b[:, 0, :]).reshape(2, 6 * D)]
    another operation x4 -> x3, other arithmetic: 14.9 us -> 0.09 us  [the longest x1 0.07 us: rope_tables(): jnp.stack([row_index[:, None] * frequency[None, :], col_index[:, None] *...]
    reduce_sum x6 -> x0, other arithmetic: 14 us -> none  [the longest x2 7.73 us: norm_back(): jnp.mean(gradient * normed, axis=-1, keepdims=True)]
  transfers between devices with their start and end apart: 10 -> 2, of which waited for: 0 -> 0; matrix products, arithmetic and copies ran while one was open for 9% -> 3% of each run, Pallas kernels for 19% -> 0%
where the time goes in v2:
time: 501 us; the launch traced here: 497 us
  Pallas kernels  376 us (75%)
  blocking collectives  78.7 us (16%)
  other arithmetic  16.1 us (3%)
  local copies, waits for them, and re-layouts  10.8 us (2%)
  matrix products  7.48 us (1%)
  starting transfers between devices  6.52 us (1%)
    pallas_call x1, Pallas kernels, backward_pass(): pl.pallas_call(backward_kernel, out_shape=[jax.ShapeDtypeStruct(*spec) fo...  221 us
    pallas_call x1, Pallas kernels, forward_pass(): pl.pallas_call(forward_kernel, out_shape=[jax.ShapeDtypeStruct(*spec) for...  155 us
    all_gather x1, blocking collectives, body_fast(): acted_all = lax.all_gather(acted_group, 'dp', axis=0, tiled=True)  31.4 us
    all_gather x1, blocking collectives, body_fast(): back_all = lax.all_gather(mod_back, 'dp', axis=0, tiled=True)  30.7 us
    unnamed x1, blocking collectives  10.4 us
  transfers between devices with their start and end apart: 2, of which 0 were waited for; matrix products, arithmetic and copies ran while one was open for 3% of the time, Pallas kernels for 0%

profile of v2, /device:TPU:0, one launch (start us, length us, event | category | flops | bytes accessed | tf_op | source)
XLA Modules:
  0.0 497.1 jit_solution(11098316557909375601)
XLA Ops:
  0.7 0.7 convert_element_type.80
  1.5 0.8 fusion.10
  2.3 6.2 %all-gather = bf16[4,2,1152]{2,1,0:T(2,128)(2,1)S(1)} all-gather(bf16[1,2,1152]{2,1,0:T(2,128)(2,1)S(1)} %fusion.10), channel_id=1, replica_groups=mesh['dp'=8,'mod'=4] {'mod'}, dimensions={0}, use_global_device_ids=true | all-gather | bytes 23040 | tf_op jit(solution)/shard_map/all_gather | solution.py:1661
  8.5 0.7 convert_element_type.82
  9.2 3.4 fusion
  12.6 0.7 all_to_all.22
  13.2 3.3 all-to-all-start
  16.5 0.9 fusion.1.refs_9_.refs_19_
  17.5 0.8 fusion.2.refs_10_.refs_20_
  18.5 1.2 pad_maximum_fusion.refs_0_
  19.7 31.4 %all_gather.10 = bf16[64,1152]{1,0:T(8,128)(2,1)S(1)} all-gather(bf16[8,1152]{1,0:T(8,128)(2,1)S(1)} %reshape.284), channel_id=1, replica_groups=mesh['dp'=8,'mod'=4] {'dp'}, dimensions={0}, use_global_device_ids=true | all-gather | bytes 165888 | tf_op jit(solution)/shard_map/all_gather | solution.py:1685
  51.2 1.4 copy.31.refs_8_.refs_17_
  52.6 1.4 copy.30.refs_7_.refs_16_
  55.4 0.6 pad_convert_fusion.refs_6_.refs_18_
  56.0 155.3 %forward_pass.1 = (bf16[4,2,144,4608]{3,2,1,0:T(8,128)(2,1)}, bf16[4,2,144,3072]{3,2,1,0:T(8,128)(2,1)}, bf16[4,2,144,3072]{3,2,1,0:T(8,128)(2,1)}, bf16[4,2,384...) custom-call(bf16[144,4608]{1,0:T(8,128)(2,1)} %pad_maximum_fusion.re, ...), custom_call_target="tpu_custom_call" | custom-call | tf_op jit(solution)/shard_map/forward_pass/pallas_call | solution.py:834
  211.4 220.6 %backward_pass.1 = (bf16[144,4608]{1,0:T(8,128)(2,1)}, bf16[144,3072]{1,0:T(8,128)(2,1)}, bf16[144,3072]{1,0:T(8,128)(2,1)}, bf16[384,1152]{1,0:T(8,128)(2,1)}, ...) custom-call(bf16[4,2,144,4608]{3,2,1,0:T(8,128)(2,1)} %get-tuple-elemen, ...), custom_call_target="tpu_custom_call" | custom-call | tf_op jit(solution)/shard_map/backward_pass/pallas_call | solution.py:1516
  432.0 1.0 slice.32
  432.9 0.9 slice.33
  434.6 3.3 all-to-all-start.1
  437.9 2.6 slice_convert_fusion
  440.5 1.9 slice_convert_fusion.1
  442.5 1.4 convert_element_type.96
  443.9 1.4 convert_element_type.97
  445.3 1.3 convert_element_type.98
  446.6 30.7 %all_gather.11 = bf16[64,1728]{1,0:T(8,128)(2,1)S(1)} all-gather(bf16[8,1728]{1,0:T(8,128)(2,1)S(1)} %all_to_all.26), channel_id=1, replica_groups=mesh['dp'=8,'mod'=4] {'dp'}, dimensions={0}, use_global_device_ids=true | all-gather | bytes 248832 | tf_op jit(solution)/shard_map/all_gather | solution.py:1686
  477.3 2.8 convolution_convert_fusion
  480.1 0.7 convert_reduce_fusion
  480.7 10.4 %all-reduce.1 = bf16[8,1152]{1,0:T(8,128)(2,1)S(1)} all-reduce(bf16[8,1152]{1,0:T(8,128)(2,1)S(1)} %convolution_convert_fusion), channel_id=2, replica_groups=mesh['dp'=8,'mod'=4] {'mod'}, use_global_device_ids=true, to_apply=%region_0.1.clone | all-reduce | flops 9216 | bytes 36864
  491.1 1.4 fusion.5
  492.5 0.7 add_multiply_fusion
  493.2 2.4 copy.38
  495.5 1.4 copy.39
  (39 shorter events, 2.2 us)
Async XLA Ops:
  9.2 9.3 %copy-start.1 = (bf16[144,3456]{1,0:T(8,128)(2,1)S(1)}, bf16[144,3456]{1,0:T(8,128)(2,1)}, u32[]{:S(2)}) copy-start(bf16[144,3456]{1,0:T(8,128)(2,1)} %param.16) | copy-start | bytes 2985988
  9.2 9.3 %copy-start.5 = (bf16[144,1152]{1,0:T(8,128)(2,1)S(1)}, bf16[144,1152]{1,0:T(8,128)(2,1)}, u32[]{:S(2)}) copy-start(bf16[144,1152]{1,0:T(8,128)(2,1)} %param.17) | copy-start | bytes 995332
  13.2 42.0 %all-to-all-start = ((bf16[4,2,1728]{2,1,0:T(2,128)(2,1)}), bf16[4,2,1728]{2,1,0:T(2,128)(2,1)S(1)}, u32[]{:S(2)}, u32[]{:S(2)}) async-start(bf16[4,2,1728]{2,1,0:T(2,128)(2,1)} %all_to_all.22), calls=%async_computation | async-start | bytes 57344 | tf_op jit(solution)/shard_map/all_to_all | solution.py:1666
  52.5 1.5 copy-start.7
  432.0 10.5 %copy-start.4 = (bf16[144,3072]{1,0:T(8,128)(2,1)S(1)}, bf16[144,3072]{1,0:T(8,128)(2,1)}, u32[]{:S(2)}) copy-start(bf16[144,3072]{1,0:T(8,128)(2,1)} %get-tuple-element.63) | copy-start | bytes 2654212
  434.6 11.9 %all-to-all-start.1 = ((bf16[2,4,1728]{2,0,1:T(2,128)(2,1)}), bf16[2,4,1728]{2,0,1:T(2,128)(2,1)S(1)}, u32[]{:S(2)}, u32[]{:S(2)}) async-start(bf16[2,4,1728]{2,0,1:T(2,128)(2,1)} %copy.34), calls=%async_computation.1 | async-start | bytes 57344 | tf_op jit(solution)/shard_map/all_to_all | solution.py:1684
  440.5 3.3 copy-start.3
  442.5 2.8 copy-start.2
  477.3 15.2 %copy-start.6 = (bf16[2,1152]{1,0:T(2,128)(2,1)S(1)}, bf16[2,1152]{1,0:T(2,128)(2,1)}, u32[]{:S(2)}) copy-start(bf16[2,1152]{1,0:T(2,128)(2,1)} %param.14) | copy-start | bytes 13828
  480.1 15.5 %copy-start = (f32[512,1152]{1,0:T(8,128)S(1)}, f32[512,1152]{1,0:T(8,128)}, u32[]{:S(2)}) copy-start(f32[512,1152]{1,0:T(8,128)} %get-tuple-element.59) | copy-start | bytes 7077892
